TPU v7x, 128 devices: a whole 4x4x4 slice. The times are simulated.
128 devices in a mesh: attn: 8 (over z, core), expert: 16 (over x, y).
Axes of the slice: x: 4, y: 4, z: 4, core: 2. Of those that a mesh axis runs over, the one named last changes fastest.
Arguments:
- queries: bfloat16 [32, 64, 576], P('attn'), may hold values from -11 to 11
- cache: bfloat16 [24576, 64, 576], P(('attn', 'expert')), may hold values from -6 to 6
- owner: int32 [24576], P(('attn', 'expert')), may hold values from 0 to 4, as said below
- uv_weight: bfloat16 [64, 512, 128], P('expert'), may hold values from -0.25 to 0.25
- out_weight: bfloat16 [8192, 7168], P('expert')
- norm_gain: float32 [7168], replicated, may hold values from 0.1 to 1.9
- expert_ids: int32 [32, 8], P('attn'), may hold values from 0 to 15, all different within a row; in each aligned block of 4 rows (0 to 3, 4 to 7, ...) at most 4 rows name the same one
- gate_values: float32 [32, 8], P('attn'), may hold values from 0.1 to 1
- gate_weight: bfloat16 [16, 7168, 2048], P('attn', None, 'expert'), may hold values from -0.0625 to 0.0625
- up_weight: bfloat16 [16, 7168, 2048], P('attn', None, 'expert'), may hold values from -0.0625 to 0.0625
- down_weight: bfloat16 [16, 2048, 7168], P('attn', 'expert'), may hold values from -0.1875 to 0.1875
Outputs:
- layer_out: bfloat16 [32, 7168], P('attn', 'expert')
Inputs may be any that keep to these rules, and one draw needn't show every extreme that they name: owner[p] names one of the 4 requests of page p's attention index, or is 4 for an empty slot; every request holds at least one page. `expert_ids`: among the rows of one attention index, no expert is named by more than 4 rows.
All inputs are finite; a program needn't handle non-finite values.
Results may differ from a plain program's by a relative error of at most 0.035.
Values may be sent and summed in bfloat16 or wider, within the bound.
A program may use at most 192 MiB of HBM per device.

v0:
```python
import jax
import jax.numpy as jnp
from jax import lax
from jax.sharding import PartitionSpec as P

NEGATIVE = -1e30
SCORE_SCALE = 192.0 ** (-0.5)
EPSILON = 1e-06
HIGHEST = lax.Precision.HIGHEST


def local_attention(queries, cache, owner, latent_width):
    row_count = queries.shape[0]
    head_count = queries.shape[1]
    pool_size = cache.shape[0]
    valid_pages = owner < row_count
    safe_owner = jnp.minimum(owner, row_count - 1)
    picked = jnp.take(queries, safe_owner, axis=0)
    scores = (
        jnp.einsum("phc,ptc->pht", picked, cache, preferred_element_type=jnp.float32) * SCORE_SCALE
    )
    page_max = jnp.where(valid_pages[:, None], jnp.max(scores, axis=2), NEGATIVE)
    member = (safe_owner[:, None] == jnp.arange(row_count, dtype=jnp.int32)[None, :]) & valid_pages[
        :, None
    ]
    row_max = jnp.max(jnp.where(member[:, :, None], page_max[:, None, :], NEGATIVE), axis=0)
    weights = jnp.where(
        valid_pages[:, None, None],
        jnp.exp(scores - jnp.take(row_max, safe_owner, axis=0)[:, :, None]),
        0.0,
    )
    probs = weights.astype(jnp.bfloat16)
    page_sum = jnp.einsum(
        "pht,ptc->phc", probs, cache[:, :, :latent_width], preferred_element_type=jnp.float32
    )
    member_float = member.astype(jnp.float32)
    totals = jnp.dot(member_float.T, jnp.sum(weights, axis=2), precision=HIGHEST)
    summed = jnp.dot(member_float.T, page_sum.reshape(pool_size, -1), precision=HIGHEST)
    return (row_max, totals, summed.reshape(row_count, head_count, latent_width))


def expert_work(arriving, gate_weight, up_weight, down_weight):
    gate_proj = jnp.einsum(
        "sjcd,jdf->sjcf", arriving, gate_weight, preferred_element_type=jnp.float32
    )
    up_proj = jnp.einsum("sjcd,jdf->sjcf", arriving, up_weight, preferred_element_type=jnp.float32)
    hidden = (jax.nn.silu(gate_proj) * up_proj).astype(jnp.bfloat16)
    return jnp.einsum("sjcf,jfd->sjcd", hidden, down_weight, preferred_element_type=jnp.float32)


def round_trip(slot_block, share_map, gate_weight, up_weight, down_weight):
    arriving = lax.all_to_all(slot_block, "attn", split_axis=0, concat_axis=0, tiled=True)
    produced = expert_work(arriving, gate_weight, up_weight, down_weight)
    reduced = lax.psum_scatter(produced, "expert", scatter_dimension=3, tiled=True)
    returned = lax.all_to_all(reduced, "attn", split_axis=0, concat_axis=0, tiled=True)
    flattened = returned.reshape(-1, returned.shape[3])
    return jnp.einsum("sr,sd->rd", share_map, flattened, precision=HIGHEST)


def on_device(
    queries,
    cache,
    owner,
    uv_weight,
    out_weight,
    norm_gain,
    expert_ids,
    gate_values,
    gate_weight,
    up_weight,
    down_weight,
):
    row_count = queries.shape[0]
    latent_width = uv_weight.shape[1]
    row_max, totals, summed = local_attention(queries, cache, owner, latent_width)
    maxima, denominators, numerators = (
        lax.all_to_all(row_max[None], "expert", split_axis=2, concat_axis=0, tiled=True),
        lax.all_to_all(totals[None], "expert", split_axis=2, concat_axis=0, tiled=True),
        lax.all_to_all(summed[None], "expert", split_axis=2, concat_axis=0, tiled=True),
    )
    peaks = jnp.max(maxima, axis=0)
    rescale = jnp.exp(maxima - peaks[None])
    total_weight = jnp.sum(rescale * denominators, axis=0)
    attended = (
        jnp.sum(rescale[:, :, :, None] * numerators, axis=0) / total_weight[:, :, None]
    ).astype(jnp.bfloat16)
    mixed_heads = jnp.einsum(
        "rhc,hcv->rhv", attended, uv_weight, preferred_element_type=jnp.float32
    )
    mixed_heads = mixed_heads.astype(jnp.bfloat16).reshape(row_count, -1)
    partial_out = jnp.dot(mixed_heads, out_weight, preferred_element_type=jnp.float32)
    attn_out = lax.psum(partial_out, "expert")
    mean_square = jnp.mean(attn_out * attn_out, axis=1, keepdims=True)
    normed = (attn_out * lax.rsqrt(mean_square + EPSILON) * norm_gain[None, :]).astype(jnp.bfloat16)
    attn_size = lax.axis_size("attn")
    expert_size = lax.axis_size("expert")
    local_experts = gate_weight.shape[0]
    expert_total = local_experts * attn_size
    top_count = expert_ids.shape[1]
    model_width = normed.shape[1]
    capacity = min(
        row_count, 2 * ((3 * row_count * top_count + 4 * expert_total - 1) // (4 * expert_total))
    )
    flat_ids = expert_ids.reshape(-1)
    matches = (flat_ids[:, None] == jnp.arange(expert_total, dtype=jnp.int32)[None, :]).astype(
        jnp.int32
    )
    earlier = jnp.cumsum(matches, axis=0) - matches
    position = jnp.sum(earlier * matches, axis=1)
    slot_index = (flat_ids * capacity + position).reshape(row_count, top_count)
    chosen = (
        jnp.arange(expert_total * capacity, dtype=jnp.int32)[:, None, None]
        == slot_index[None, :, :]
    )
    pick_map = jnp.any(chosen, axis=2).astype(jnp.bfloat16)
    weight_map = jnp.sum(jnp.where(chosen, gate_values[None, :, :], 0.0), axis=2)
    outgoing = jnp.dot(pick_map, normed, preferred_element_type=jnp.float32).astype(jnp.bfloat16)
    outgoing = outgoing.reshape(attn_size, local_experts, capacity, model_width)
    weight_grid = weight_map.reshape(attn_size, local_experts, capacity, row_count)
    share_map = weight_grid.reshape(-1, row_count)
    section_sum = round_trip(outgoing, share_map, gate_weight, up_weight, down_weight)
    column_width = model_width // expert_size
    attn_columns = lax.dynamic_slice_in_dim(
        attn_out, lax.axis_index("expert") * column_width, column_width, 1
    )
    return (attn_columns + section_sum).astype(jnp.bfloat16)


def solution(mesh):
    placed = (
        P("attn", None, None),
        P(("attn", "expert"), None, None),
        P(("attn", "expert")),
        P("expert", None, None),
        P("expert", None),
        P(),
        P("attn", None),
        P("attn", None),
        P("attn", None, "expert"),
        P("attn", None, "expert"),
        P("attn", "expert", None),
    )
    return jax.shard_map(
        on_device, mesh=mesh, in_specs=placed, out_specs=P("attn", "expert"), check_vma=False
    )
```

profile of v0, /device:TPU:1, one launch (start us, length us, event | category | flops | bytes accessed | tf_op | source)
XLA Modules:
  0.0 384.2 jit_solution(11106621884005514824)
XLA Ops:
  8.0 10.4 %gather_fusion = bf16[192,64,576]{2,1,0:T(8,128)(2,1)} fusion(bf16[4,64,576]{2,1,0:T(8,128)(2,1)} %param.11, s32[1024]{0:T(1024)S(1)} %pad_clamp_fusion), kind=kCustom, calls=%fused_computation | custom fusion | bytes 28312320 | tf_op jit(solution)/shard_map/jit(_take)/gather | solution.py:18
  18.4 15.5 %fusion.3 = f32[192,64,64]{1,2,0:T(8,128)} fusion(bf16[192,64,576]{2,1,0:T(8,128)(2,1)} %param.12, bf16[192,64,576]{2,1,0:T(8,128)(2,1)} %gather_fusion, pred[192]{0:T(512)(128)(4,1)S(1)} %get-tuple-element.12), kind=kOutput, calls=%fused_computation.5 | convolution fusion | flops 913047552 | bytes 31457472 | tf_op jit(solution)/shard_map/phc,ptc->pht/dot_general | solution.py:20
  33.8 7.6 %copy.80 = f32[192,64,64]{0,2,1:T(8,128)} copy(f32[192,64,64]{1,2,0:T(8,128)} %fusion.3) | data formatting | bytes 6291456 | tf_op jit(solution)/shard_map/phc,ptc->pht/dot_general | solution.py:20
  41.4 2.9 multiply_reduce_fusion
  45.6 3.5 fusion.14
  49.8 7.4 %all-to-all-start.2 = ((f32[1,4,64]{1,0,2:T(1,128)}), f32[1,4,64]{1,0,2:T(1,128)S(1)}, u32[]{:S(2)}, u32[]{:S(2)}) async-start(f32[1,4,64]{1,0,2:T(1,128)} %bitcast.38), calls=%async_computation.2 | async-start | bytes 65536 | tf_op jit(solution)/shard_map/all_to_all | solution.py:78
  57.2 3.8 copy.87
  61.0 17.2 %fusion.6 = f32[192,64,512]{2,1,0:T(8,128)} fusion(bf16[192,64,64]{2,1,0:T(8,128)(2,1)} %copy.87, bf16[192,64,576]{2,1,0:T(8,128)(2,1)} %param.12), kind=kOutput, calls=%fused_computation.8 | convolution fusion | flops 805306368 | bytes 40894464 | tf_op jit(solution)/shard_map/pht,ptc->phc/dot_general | solution.py:33
  79.0 6.7 %all-to-all-start = ((f32[1,4,64]{1,0,2:T(1,128)}), f32[1,4,64]{1,0,2:T(1,128)S(1)}, u32[]{:S(2)}, u32[]{:S(2)}) async-start(f32[1,4,64]{1,0,2:T(1,128)} %copy.83), calls=%async_computation | async-start | bytes 65536 | tf_op jit(solution)/shard_map/all_to_all | solution.py:77
  85.6 28.2 %fusion.16 = f32[1,4,64,512]{3,1,0,2:T(4,128)} fusion(pred[192,4]{0,1:T(4,128)(4,1)S(1)} %fusion.38, f32[24,8,64,512]{3,2,1,0:T(8,128)} %bitcast.99), kind=kOutput, calls=%fused_computation.22 | convolution fusion | flops 301989888 | bytes 25690880 | tf_op jit(solution)/shard_map/dot_general | solution.py:38
  114.0 6.7 %all-to-all-start.1 = ((f32[1,4,64,512]{3,1,0,2:T(4,128)}), f32[1,4,64,512]{3,1,0,2:T(4,128)S(1)}, u32[]{:S(2)}, u32[]{:S(2)}) async-start(f32[1,4,64,512]{3,1,0,2:T(4,128)} %fusion.16), calls=%async_computation.1 | async-start | bytes 1048576 | tf_op jit(solution)/shard_map/all_to_all | solution.py:79
  122.1 7.7 %all-to-all-done.1 = f32[1,4,64,512]{3,1,0,2:T(4,128)S(1)} async-done(((f32[1,4,64,512]{3,1,0,2:T(4,128)}), f32[1,4,64,512]{3,1,0,2:T(4,128)S(1)}, u32[]{:S(2)}, u32[]{:S(2)}) %all-to-all-start.1) | async-done | bytes 524320 | tf_op jit(solution)/shard_map/all_to_all | solution.py:79
  130.0 5.0 %fusion.23 = f32[4,7168]{1,0:T(4,128)} fusion(bf16[512,7168]{1,0:T(8,128)(2,1)} %param.15, bf16[4,512,128]{2,1,0:T(8,128)(2,1)S(1)} %copy-done, f32[4,4,512]{2,0,1:T(4,128)S(1)} %multiply_reduce_fusion.1, f32[4,4]{0,1:T(4,128)S(1)} %copy.92), kind=kOutput, calls=%fused_computation.29 | convolution fusion | flops 31475712 | bytes 8011840 | tf_op jit(solution)/shard_map/dot_general | solution.py:91
  135.2 81.8 %all-reduce.2.cloned.1.call-done = f32[4,7168]{1,0:T(4,128)} async-done(((f32[4,7168]{1,0:T(4,128)}), f32[4,7168]{1,0:T(4,128)}) %all-reduce.2.cloned.1.call-update) | async-done | bytes 114704 | tf_op jit(solution)/shard_map/psum | solution.py:92
  219.7 20.8 %all_to_all.64 = bf16[8,2,4,7168]{3,2,1,0:T(4,128)(2,1)S(1)} all-to-all(bf16[8,2,4,7168]{3,2,1,0:T(4,128)(2,1)S(1)} %reshape.116), channel_id=1, replica_groups=mesh['attn'=8,'expert'=16] {'attn'}, dimensions={0} | all-to-all | bytes 1835008 | tf_op jit(solution)/shard_map/all_to_all | solution.py:52
  240.5 3.0 fusion.10
  245.0 18.9 %copy.103 = f32[8,2,4,7168]{0,2,1,3:T(4,128)} copy(f32[8,2,4,7168]{3,0,2,1:T(8,128)S(1)} %convolution_bitcast_fusion) | data formatting | bytes 3670016
  263.9 24.2 %reshape.140 = f32[7168,64]{1,0:T(8,128)} reshape(f32[7168,2,4,8]{3,2,1,0:T(4,128)} %bitcast.100) | data formatting | bytes 3670016
  288.1 71.8 %reduce-scatter.4.cloned.1.call-done = f32[448,64]{1,0:T(8,128)} async-done(((f32[7168,64]{1,0:T(8,128)}), f32[448,64]{1,0:T(8,128)}) %reduce-scatter.4.cloned.1.call-update) | async-done | bytes 114704
  360.0 2.2 reshape.141
  362.1 1.6 copy.97
  363.7 6.8 %all-to-all-start.4 = ((f32[8,2,4,448]{3,2,1,0:T(4,128)}), f32[8,2,4,448]{3,2,1,0:T(4,128)S(1)}, u32[]{:S(2)}, u32[]{:S(2)}) async-start(f32[8,2,4,448]{3,2,1,0:T(4,128)} %copy.97), calls=%async_computation.4 | async-start | bytes 262144 | tf_op jit(solution)/shard_map/all_to_all | solution.py:55
  370.6 5.2 %all-to-all-done.4 = f32[8,2,4,448]{3,2,1,0:T(4,128)S(1)} async-done(((f32[8,2,4,448]{3,2,1,0:T(4,128)}), f32[8,2,4,448]{3,2,1,0:T(4,128)S(1)}, u32[]{:S(2)}, u32[]{:S(2)}) %all-to-all-start.4) | async-done | bytes 114720 | tf_op jit(solution)/shard_map/all_to_all | solution.py:55
  375.9 1.5 fusion.19
  (53 shorter events, 10.3 us)
Async XLA Ops:
  6.5 123.5 %copy-start = (bf16[4,512,128]{2,1,0:T(8,128)(2,1)S(1)}, bf16[4,512,128]{2,1,0:T(8,128)(2,1)}, u32[]{:S(2)}) copy-start(bf16[4,512,128]{2,1,0:T(8,128)(2,1)} %param.14) | copy-start | bytes 1572868
  49.8 29.1 %all-to-all-start.2 = ((f32[1,4,64]{1,0,2:T(1,128)}), f32[1,4,64]{1,0,2:T(1,128)S(1)}, u32[]{:S(2)}, u32[]{:S(2)}) async-start(f32[1,4,64]{1,0,2:T(1,128)} %bitcast.38), calls=%async_computation.2 | async-start | bytes 65536 | tf_op jit(solution)/shard_map/all_to_all | solution.py:78
  79.0 35.0 %all-to-all-start = ((f32[1,4,64]{1,0,2:T(1,128)}), f32[1,4,64]{1,0,2:T(1,128)S(1)}, u32[]{:S(2)}, u32[]{:S(2)}) async-start(f32[1,4,64]{1,0,2:T(1,128)} %copy.83), calls=%async_computation | async-start | bytes 65536 | tf_op jit(solution)/shard_map/all_to_all | solution.py:77
  85.6 28.3 %copy-start.3 = (s32[4,8]{1,0:T(4,128)S(1)}, s32[4,8]{1,0:T(4,128)}, u32[]{:S(2)}) copy-start(s32[4,8]{1,0:T(4,128)} %param.17) | copy-start | bytes 388
  114.0 15.9 %all-to-all-start.1 = ((f32[1,4,64,512]{3,1,0,2:T(4,128)}), f32[1,4,64,512]{3,1,0,2:T(4,128)S(1)}, u32[]{:S(2)}, u32[]{:S(2)}) async-start(f32[1,4,64,512]{3,1,0,2:T(4,128)} %fusion.16), calls=%async_computation.1 | async-start | bytes 1048576 | tf_op jit(solution)/shard_map/all_to_all | solution.py:79
  120.6 96.3 %all-reduce.2.cloned.1.call-start = ((), (), s32[]{:S(2)}) async-start(), calls=%async_computation.6 | async-start | bytes 229376 | tf_op jit(solution)/shard_map/psum | solution.py:92
  130.0 88.0 %copy-start.2 = (f32[7168]{0:T(1024)S(1)}, f32[7168]{0:T(1024)}, u32[]{:S(2)}) copy-start(f32[7168]{0:T(1024)} %param.16) | copy-start | bytes 86020
  135.0 224.9 %reduce-scatter.4.cloned.1.call-start = ((), (), s32[]{:S(2)}) async-start(), calls=%async_computation.7 | async-start | bytes 3899392
  219.7 23.8 %copy-start.5 = (bf16[2,7168,128]{2,1,0:T(8,128)(2,1)S(1)}, bf16[2,7168,128]{2,1,0:T(8,128)(2,1)}, u32[]{:S(2)}) copy-start(bf16[2,7168,128]{2,1,0:T(8,128)(2,1)} %param.19) | copy-start | bytes 11010052
  240.5 3.8 copy-start.1
  288.1 82.4 %copy-start.4 = (f32[4,8]{1,0:T(4,128)S(1)}, f32[4,8]{1,0:T(4,128)}, u32[]{:S(2)}) copy-start(f32[4,8]{1,0:T(4,128)} %param.18) | copy-start | bytes 388
  363.7 12.1 %all-to-all-start.4 = ((f32[8,2,4,448]{3,2,1,0:T(4,128)}), f32[8,2,4,448]{3,2,1,0:T(4,128)S(1)}, u32[]{:S(2)}, u32[]{:S(2)}) async-start(f32[8,2,4,448]{3,2,1,0:T(4,128)} %copy.97), calls=%async_computation.4 | async-start | bytes 262144 | tf_op jit(solution)/shard_map/all_to_all | solution.py:55
Sparse Core Ops, SparseCore 0:
  135.2 81.7 all-reduce.1
  288.3 71.6 reduce-scatter.3
where the time goes:
time: 385 us; the launch traced here: 384 us
  waiting for transfers between devices  167 us (43%)
  matrix products  73.9 us (19%)
  local copies, waits for them, and re-layouts  71.5 us (19%)
  starting transfers between devices  27.8 us (7%)
  blocking collectives  20.8 us (5%)
  between operations  13.6 us (4%)
  other arithmetic  9.93 us (3%)
    psum x1, waiting for transfers between devices, on_device(): attn_out = lax.psum(partial_out, 'expert')  81.8 us
    unnamed x3, waiting for transfers between devices  71.8 us
    unnamed x16, local copies, waits for them, and re-layouts  45.4 us
    dot_general x1, matrix products, local_attention(): jnp.dot(member_float.T, page_sum.reshape(pool_size, -1), precision=HIGHEST)  28.2 us
    all_to_all x1, blocking collectives, round_trip(): lax.all_to_all(slot_block, 'attn', split_axis=0, concat_axis=0, tiled=True)  20.8 us
    dot_general x1, matrix products, local_attention(): jnp.einsum('pht,ptc->phc', probs, cache[:, :, :latent_width], preferred_e...  17.2 us
    dot_general x1, matrix products, local_attention(): jnp.einsum('phc,ptc->pht', picked, cache, preferred_element_type=jnp.floa...  15.5 us
    gather x1, local copies, waits for them, and re-layouts, local_attention(): picked = jnp.take(queries, safe_owner, axis=0)  10.4 us
  transfers between devices with their start and end apart: 6, of which 4 were waited for; matrix products, arithmetic and copies ran while one was open for 13% of the time, Pallas kernels for 0%

commit v1 on v0

v1 whole, which is shorter than its diff:
```python
import functools
import jax
import jax.numpy as jnp
from jax import lax
from jax.experimental import pallas as pl
from jax.experimental.pallas import tpu as pltpu
from jax.sharding import PartitionSpec as P

SCORE_SCALE = 192.0 ** (-0.5)
LOG2E = 1.4426950408889634
EPSILON = 1e-06
MASKED = -1e30
FLOOR = -1e20
F32 = jnp.float32
BF16 = jnp.bfloat16
MESH = pl.DeviceIdType.MESH

NE = 16
CHUNK_PAGES = 16


def split_bf16(value, parts):
    out = []
    for _ in range(parts):
        piece = value.astype(BF16).astype(F32)
        out.append(piece)
        value = value - piece
    return out


def attention_kernel(owner, q_ref, cache_ref, out_ref, q_rows, m_ref, l_ref, acc_ref):
    step = pl.program_id(0)
    rows = 256
    tokens = CHUNK_PAGES * 64

    @pl.when(step == 0)
    def _():
        i = lax.broadcasted_iota(jnp.int32, (rows, rows), 0)
        j = lax.broadcasted_iota(jnp.int32, (rows, rows), 1)
        order = (j == (i % 4) * 64 + i // 4).astype(F32).astype(BF16)
        q_rows[...] = jnp.dot(
            order, q_ref[...].reshape(rows, 576), preferred_element_type=F32
        ).astype(BF16)
        m_ref[...] = jnp.full_like(m_ref, FLOOR)
        l_ref[...] = jnp.zeros_like(l_ref)
        acc_ref[...] = jnp.zeros_like(acc_ref)

    lane = lax.broadcasted_iota(jnp.int32, (8, 128), 1)
    request = lax.broadcasted_iota(jnp.int32, (8, 128), 0) % 4
    bias = []
    for pair in range(CHUNK_PAGES // 2):
        first = owner[step * CHUNK_PAGES + 2 * pair]
        second = owner[step * CHUNK_PAGES + 2 * pair + 1]
        bias.append(jnp.where(jnp.where(lane < 64, first, second) == request, 0.0, MASKED))
    bias = jnp.concatenate(bias, axis=1)
    keys = cache_ref[...].reshape(tokens, 576)
    scores = lax.dot_general(
        q_rows[...], keys, (((1,), (1,)), ((), ())), preferred_element_type=F32
    )
    scores = scores.reshape(32, 8, tokens) * (SCORE_SCALE * LOG2E) + bias[None]
    scores = scores.reshape(rows, tokens)
    m_old = m_ref[...]
    m_new = jnp.maximum(m_old, jnp.max(scores, axis=1, keepdims=True))
    alpha = jnp.exp2(m_old - m_new)
    probs = jnp.exp2(scores - m_new[:, :1])
    l_ref[...] = l_ref[...] * alpha + jnp.sum(probs, axis=1, keepdims=True)
    m_ref[...] = m_new
    acc_ref[...] = acc_ref[...] * alpha[:, :1] + jnp.dot(
        probs.astype(BF16), keys[:, :512], preferred_element_type=F32
    )

    @pl.when(step == pl.num_programs(0) - 1)
    def _():
        total = l_ref[...]
        safe = jnp.where(total > 0.0, total, 1.0)
        lse = jnp.where(total > 0.0, m_ref[...] + jnp.log2(safe), FLOOR)
        wide = lax.broadcasted_iota(jnp.int32, (rows, 128), 1)
        pieces = split_bf16(lse, 3)
        coded = jnp.zeros((rows, 128), F32)
        for at, piece in enumerate(pieces):
            coded = jnp.where(wide == at, piece, coded)
        value = (acc_ref[...] / safe[:, :1]).astype(BF16)
        out_ref[:, :, :512] = value.reshape(16, 16, 512)
        out_ref[:, :, 512:] = coded.astype(BF16).reshape(16, 16, 128)


def attention(owner, queries, cache):
    pages = cache.shape[0]
    return pl.pallas_call(
        attention_kernel,
        out_shape=jax.ShapeDtypeStruct((16, 16, 640), BF16),
        grid_spec=pltpu.PrefetchScalarGridSpec(
            num_scalar_prefetch=1,
            grid=(pages // CHUNK_PAGES,),
            in_specs=[
                pl.BlockSpec((4, 64, 576), lambda i, o: (0, 0, 0)),
                pl.BlockSpec((CHUNK_PAGES, 64, 576), lambda i, o: (i, 0, 0)),
            ],
            out_specs=pl.BlockSpec((16, 16, 640), lambda i, o: (0, 0, 0)),
            scratch_shapes=[
                pltpu.VMEM((256, 576), BF16),
                pltpu.VMEM((256, 128), F32),
                pltpu.VMEM((256, 128), F32),
                pltpu.VMEM((256, 512), F32),
            ],
        ),
        compiler_params=pltpu.CompilerParams(vmem_limit_bytes=32 << 20),
        name="attention",
    )(owner, queries, cache)


def window_tile(e):
    return (e // 2) * 7 + (e % 2) * 3


def fold(rows4):
    return jnp.concatenate([rows4[:, 128 * j : 128 * j + 128] for j in range(4)], axis=0)


def layer_kernel(
    partial_hbm, uv_hbm, outw_hbm, gain_hbm, ids_ref, values_ref, gate_hbm, up_hbm, down_hbm,
    out_ref,
    uv, outw, gain, gate, up, down,
    part_recv, term_send, term_recv, z_send, z_recv, x_mine, x_buf,
    pair_send, pair_keep, pair_recv, plane_send, plane_recv, last_send, last_recv,
    load_sem, s1, r1, s2, r2, s3, r3, s4, r4, s5, r5, s6, r6, s7, r7, s8, r8,
):
    a = lax.axis_index("attn")
    e = lax.axis_index("expert")
    z = a // 2
    core = a % 2
    odd = e % 2
    sibling = {"attn": z * 2 + (1 - core)}

    def plane_peer(k):
        return lax.rem(e + k, NE)

    def z_peer(k):
        return lax.rem(z + k, 4)

    def remote(src, dst, send, recv, device):
        return pltpu.make_async_remote_copy(
            src_ref=src, dst_ref=dst, send_sem=send, recv_sem=recv,
            device_id=device, device_id_type=MESH,
        )

    loads = [
        pltpu.make_async_copy(src, dst, load_sem.at[n])
        for n, (src, dst) in enumerate(
            [(partial_hbm.at[e], part_recv.at[15]), (uv_hbm, uv), (outw_hbm, outw), (gain_hbm, gain),
             (gate_hbm, gate), (up_hbm, up), (down_hbm, down)]
        )
    ]
    for load in loads:
        load.start()

    barrier = pltpu.get_barrier_semaphore()
    for k in range(1, NE):
        pl.semaphore_signal(barrier, inc=1, device_id={"expert": plane_peer(k)}, device_id_type=MESH)
    for k in range(1, 4):
        pl.semaphore_signal(barrier, inc=1, device_id={"attn": z_peer(k) * 2 + core}, device_id_type=MESH)
    pl.semaphore_signal(barrier, inc=1, device_id=sibling, device_id_type=MESH)
    pl.semaphore_wait(barrier, 19)

    sends = []
    first = []
    for k in range(1, NE):
        to = plane_peer(k)
        copy = remote(partial_hbm.at[to], part_recv.at[k - 1], s1.at[k - 1], r1.at[k - 1], {"expert": to})
        copy.start()
        first.append(copy)
    sends += first

    lane = lax.broadcasted_iota(jnp.int32, (16, 128), 1)
    row = lax.broadcasted_iota(jnp.int32, (16, 128), 0)
    spot = lane % 64
    ids = jnp.concatenate([ids_ref[...]] * 4, axis=0)
    values = jnp.concatenate([values_ref[...]] * 4, axis=0)
    expert_at = jnp.where(spot < 32, spot - 16, spot - 32)
    expert_at = jnp.where((spot >= 16) & (spot < 48), expert_at, -1)
    routing = jnp.zeros((16, 128), F32)
    for k in range(8):
        routing += jnp.where(ids[:, k : k + 1] == expert_at, values[:, k : k + 1], 0.0)
    high, low = split_bf16(routing, 2)
    coded = jnp.where(spot < 32, high, low)
    side = (row // 4 == 3 * (1 - odd)) & (lane // 64 == 1 - odd)

    loads[0].wait()
    for copy in first:
        copy.wait_recv()

    lse = [jnp.sum(part_recv[s, :, 512:].astype(F32), axis=1, keepdims=True) for s in range(NE)]
    peak = functools.reduce(jnp.maximum, lse)
    total = jnp.zeros_like(peak)
    summed = jnp.zeros((16, 512), F32)
    for s in range(NE):
        weight = jnp.exp2(lse[s] - peak)
        total += weight
        summed += weight * part_recv[s, :, :512].astype(F32)
    attended = (summed / total).astype(BF16)
    loads[1].wait()
    mixed = []
    for h in range(4):
        mapped = jnp.dot(attended, uv[h], preferred_element_type=F32)
        mixed.append(jnp.concatenate([mapped[4 * h : 4 * h + 4]] * 4, axis=0))
    mixed = jnp.concatenate(mixed, axis=1).astype(BF16)
    loads[2].wait()

    def terms(to):
        start = pl.multiple_of(window_tile(to) * 128, 128)
        wide = jnp.dot(mixed, outw[:, pl.ds(start, 512)], preferred_element_type=F32)
        folded = jnp.zeros((16, 128), F32)
        for j in range(4):
            folded = jnp.where(row // 4 == j, wide[:, 128 * j : 128 * j + 128], folded)
        return folded

    second = []
    for k in range(1, NE):
        to = plane_peer(k)
        term_send[k - 1] = terms(to).astype(BF16)
        copy = remote(term_send.at[k - 1], term_recv.at[k - 1], s2.at[k - 1], r2.at[k - 1], {"expert": to})
        copy.start()
        second.append(copy)
    sends += second
    attn_out = terms(e)
    for copy in second:
        copy.wait_recv()
    for k in range(NE - 1):
        attn_out += term_recv[k].astype(F32)

    loads[3].wait()
    gains = gain[pl.ds(window_tile(e), 4), :]
    gains = jnp.concatenate([jnp.broadcast_to(gains[j : j + 1], (4, 128)) for j in range(4)], axis=0)
    squares = jnp.sum(jnp.where(side, 0.0, attn_out * attn_out), axis=1, keepdims=True)
    squares = squares[0:4] + squares[4:8] + squares[8:12] + squares[12:16]
    squares = jnp.broadcast_to(jnp.concatenate([squares] * 4, axis=0), (16, 128))
    high, low = split_bf16(squares, 2)
    coded = jnp.where(spot == 0, high, jnp.where(spot == 1, low, coded))
    mine = jnp.where(side, coded, attn_out * gains).astype(BF16)
    z_send[...] = mine
    third = []
    for k in range(1, 4):
        copy = remote(z_send, z_recv.at[z], s3.at[k - 1], r3.at[z], {"attn": z_peer(k) * 2 + core})
        copy.start()
        third.append(copy)
    sends += third
    z_recv[z] = mine
    for k in range(1, 4):
        remote(z_send, z_recv.at[z_peer(k)], s3.at[k - 1], r3.at[z_peer(k)], sibling).wait_recv()
    blocks = [z_recv[n].astype(F32) for n in range(4)]
    wide = jnp.concatenate(
        [jnp.concatenate([blocks[n][4 * j : 4 * j + 4] for n in range(4)], axis=0) for j in range(4)],
        axis=1,
    )
    x_mine[...] = wide.astype(BF16)
    x_buf[e, core] = wide.astype(BF16)
    for k in range(1, NE):
        to = plane_peer(k)
        copy = remote(x_mine, x_buf.at[e, core], s4.at[k - 1], r4.at[e], {"expert": to})
        copy.start()
        sends.append(copy)
    copy = remote(x_mine, x_buf.at[e, core], s5.at[0], r5.at[e], sibling)
    copy.start()
    sends.append(copy)
    for k in range(1, NE):
        source = plane_peer(k)
        block = x_buf.at[source, core]
        remote(x_mine, block, s4.at[k - 1], r4.at[source], sibling).wait_recv()
        copy = remote(block, block, s5.at[k], r5.at[source], sibling)
        copy.start()
        sends.append(copy)

    for load in loads[4:6]:
        load.wait()
    products = [jnp.zeros((32, 256), F32) for _ in range(2)]
    squares = jnp.zeros((32, 1), F32)
    lane32 = lax.broadcasted_iota(jnp.int32, (32, 128), 1)
    for k in range(8):
        pair = lax.rem(e // 2 + k, 8)
        for half in range(2):
            source = pair * 2 + half
            block = x_buf.at[source, 1 - core]
            remote(x_mine, block, s5.at[0], r5.at[source], sibling).wait_recv()
        even = x_buf[pair * 2].reshape(32, 512)
        odds = x_buf[pair * 2 + 1].reshape(32, 512)
        middle = jnp.where(lane32 < 64, even[:, 384:], odds[:, :128])
        extra = jnp.where(lane32 < 64, odds[:, :128], even[:, 384:])
        squares += jnp.sum(jnp.where(lane32 % 64 < 2, extra.astype(F32), 0.0), axis=1, keepdims=True)
        x = jnp.concatenate([even[:, :384], middle, odds[:, 128:]], axis=1)
        at = pl.ds(pl.multiple_of(pair * 896, 128), 896)
        for j in range(2):
            weights = jnp.concatenate([gate[j, at, :], up[j, at, :]], axis=1)
            products[j] += jnp.dot(x, weights, preferred_element_type=F32)
        if k == 0:
            base = jnp.where(odd == 1, 0, 64)
            share = []
            for j in range(2):
                number = 2 * a + j
                chosen = (lane32 == base + 16 + number) | (lane32 == base + 32 + number)
                share.append(jnp.sum(jnp.where(chosen, extra.astype(F32), 0.0), axis=1, keepdims=True))
    scale = lax.rsqrt(squares / 7168.0 + EPSILON)
    hidden = []
    for j in range(2):
        g = products[j][:, :128] * scale
        u = products[j][:, 128:] * scale
        hidden.append(g / (1.0 + jnp.exp(-g)) * u * share[j])
    hidden = jnp.concatenate(hidden, axis=1).astype(BF16)

    loads[6].wait()
    swap = []
    for k in range(8):
        pair = lax.rem(e // 2 + k, 8)
        at = pl.ds(pl.multiple_of(pair * 896, 128), 896)
        produced = jnp.dot(hidden, down[:, at], preferred_element_type=F32)
        top, bottom = produced[:16], produced[16:]
        pair_keep[k] = jnp.where(core == 0, top, bottom)
        pair_send[k] = jnp.where(core == 0, bottom, top).astype(BF16)
        copy = remote(pair_send.at[k], pair_recv.at[k], s6.at[k], r6.at[k], sibling)
        copy.start()
        swap.append(copy)
    sends += swap
    seventh = []
    for k in range(8):
        pair = lax.rem(e // 2 + k, 8)
        swap[k].wait_recv()
        both = pair_keep[k] + pair_recv[k].astype(F32)
        lower, upper = both[:, :512], both[:, 384:]
        if k == 0:
            own = jnp.where(odd == 1, upper, lower)
            plane_send[0] = jnp.where(odd == 1, lower, upper).astype(BF16)
            targets = [(0, pair * 2 + (1 - odd))]
        else:
            plane_send[2 * k - 1] = lower.astype(BF16)
            plane_send[2 * k] = upper.astype(BF16)
            targets = [(2 * k - 1, pair * 2), (2 * k, pair * 2 + 1)]
        for at, to in targets:
            slot = lax.rem(e - to + NE, NE) - 1
            copy = remote(plane_send.at[at], plane_recv.at[slot], s7.at[at], r7.at[slot], {"expert": to})
            copy.start()
            sends.append(copy)
    for k in range(NE - 1):
        remote(plane_send.at[0], plane_recv.at[k], s7.at[0], r7.at[k], sibling).wait_recv()
        own += plane_recv[k].astype(F32)

    for n in range(4):
        last_send[n] = fold(own[4 * n : 4 * n + 4]).astype(BF16)
    last = []
    for k in range(1, 4):
        to = z_peer(k)
        copy = remote(last_send.at[to], last_recv.at[k - 1], s8.at[k - 1], r8.at[k - 1], {"attn": to * 2 + core})
        copy.start()
        last.append(copy)
    sends += last
    result = attn_out + last_send[z].astype(F32)
    for copy in last:
        copy.wait_recv()
    for k in range(3):
        result += last_recv[k].astype(F32)
    out_ref[...] = jnp.concatenate([result[4 * j : 4 * j + 4] for j in range(4)], axis=1).astype(BF16)
    for copy in sends:
        copy.wait_send()


def layer(partial, uv, outw, gain, ids, values, gate, up, down):
    dma = pltpu.SemaphoreType.DMA
    hbm = pl.BlockSpec(memory_space=pl.ANY)
    vmem = pl.BlockSpec(memory_space=pltpu.VMEM)
    return pl.pallas_call(
        layer_kernel,
        out_shape=jax.ShapeDtypeStruct((4, 512), BF16),
        in_specs=[hbm, hbm, hbm, hbm, vmem, vmem, hbm, hbm, hbm],
        out_specs=vmem,
        scratch_shapes=[
            pltpu.VMEM(uv.shape, BF16),
            pltpu.VMEM(outw.shape, BF16),
            pltpu.VMEM(gain.shape, F32),
            pltpu.VMEM(gate.shape, BF16),
            pltpu.VMEM(up.shape, BF16),
            pltpu.VMEM(down.shape, BF16),
            pltpu.VMEM((16, 16, 640), BF16),
            pltpu.VMEM((15, 16, 128), BF16),
            pltpu.VMEM((15, 16, 128), BF16),
            pltpu.VMEM((16, 128), BF16),
            pltpu.VMEM((4, 16, 128), BF16),
            pltpu.VMEM((16, 512), BF16),
            pltpu.VMEM((16, 2, 16, 512), BF16),
            pltpu.VMEM((8, 16, 896), BF16),
            pltpu.VMEM((8, 16, 896), F32),
            pltpu.VMEM((8, 16, 896), BF16),
            pltpu.VMEM((15, 16, 512), BF16),
            pltpu.VMEM((15, 16, 512), BF16),
            pltpu.VMEM((4, 16, 128), BF16),
            pltpu.VMEM((3, 16, 128), BF16),
            dma((7,)),
            dma((15,)), dma((15,)),
            dma((15,)), dma((15,)),
            dma((3,)), dma((4,)),
            dma((15,)), dma((16,)),
            dma((16,)), dma((16,)),
            dma((8,)), dma((8,)),
            dma((15,)), dma((15,)),
            dma((3,)), dma((3,)),
        ],
        compiler_params=pltpu.CompilerParams(
            collective_id=0, has_side_effects=True, vmem_limit_bytes=48 << 20
        ),
        name="layer",
    )(partial, uv, outw, gain, ids, values, gate, up, down)


def on_device(
    queries, cache, owner, uv_weight, out_weight, norm_gain, expert_ids, gate_values,
    gate_weight, up_weight, down_weight,
):
    partial = attention(owner, queries, cache)
    wide = layer(
        partial, uv_weight, out_weight, norm_gain.reshape(56, 128), expert_ids, gate_values,
        gate_weight, up_weight, down_weight.reshape(256, 7168),
    )
    start = (lax.axis_index("expert") % 2) * 64
    return lax.dynamic_slice_in_dim(wide, start, 448, 1)


def solution(mesh):
    placed = (
        P("attn", None, None),
        P(("attn", "expert"), None, None),
        P(("attn", "expert")),
        P("expert", None, None),
        P("expert", None),
        P(),
        P("attn", None),
        P("attn", None),
        P("attn", None, "expert"),
        P("attn", None, "expert"),
        P("attn", "expert", None),
    )
    return jax.shard_map(
        on_device, mesh=mesh, in_specs=placed, out_specs=P("attn", "expert"), check_vma=False
    )
```

time: 385 us -> 70.4 us (0.18)
  waiting for transfers between devices: 167 us -> 0 us
  matrix products: 73.9 us -> 0 us
  local copies, waits for them, and re-layouts: 71.5 us -> 7.81 us
  Pallas kernels: 0 us -> 62.1 us
  starting transfers between devices: 27.8 us -> 0 us
  blocking collectives: 20.8 us -> 0 us
  between operations: 13.6 us -> 0.09 us
  other arithmetic: 9.93 us -> 0 us
    psum x1 -> x0, waiting for transfers between devices: 81.8 us -> none  [on_device(): attn_out = lax.psum(partial_out, 'expert')]
    dot_general x10 -> x0, matrix products: 73.9 us -> none  [the longest x1 28.2 us: local_attention(): jnp.dot(member_float.T, page_sum.reshape(pool_size, -1), precision=HIGHEST)]
    unnamed x3 -> x0, waiting for transfers between devices: 71.8 us -> none
    pallas_call x0 -> x2, Pallas kernels: none -> 62.1 us  [the longest x1 46 us: layer(): pl.pallas_call(layer_kernel, out_shape=jax.ShapeDtypeStruct((4, 512), BF1...]
    unnamed x16, local copies, waits for them, and re-layouts: 45.4 us -> 7.14 us
    all_to_all x4 -> x0, starting transfers between devices: 27.5 us -> none  [the longest x1 7.39 us: on_device(): lax.all_to_all(totals[None], 'expert', split_axis=2, concat_axis=0, tiled...]
    all_to_all x1 -> x0, blocking collectives: 20.8 us -> none  [round_trip(): lax.all_to_all(slot_block, 'attn', split_axis=0, concat_axis=0, tiled=True)]
    all_to_all x4 -> x0, waiting for transfers between devices: 12.9 us -> none  [the longest x1 7.74 us: on_device(): lax.all_to_all(summed[None], 'expert', split_axis=2, concat_axis=0, tiled...]
  transfers between devices with their start and end apart: 6 -> 0, of which waited for: 4 -> 0; matrix products, arithmetic and copies ran while one was open for 13% -> 0% of each run, Pallas kernels for 0% -> 0%
where the time goes in v1:
time: 70.4 us; the launch traced here: 70 us
  Pallas kernels  62.1 us (88%)
  local copies, waits for them, and re-layouts  7.81 us (11%)
    pallas_call x1, Pallas kernels, layer(): pl.pallas_call(layer_kernel, out_shape=jax.ShapeDtypeStruct((4, 512), BF1...  46 us
    pallas_call x1, Pallas kernels, attention(): pl.pallas_call(attention_kernel, out_shape=jax.ShapeDtypeStruct((16, 16,...  16.2 us
    unnamed x16, local copies, waits for them, and re-layouts  7.14 us

profile of v1, /device:TPU:1, one launch (start us, length us, event | category | flops | bytes accessed | tf_op | source)
XLA Modules:
  0.0 70.0 jit_solution(4846387500376920945)
XLA Ops:
  0.0 0.0 copy-start
  0.0 5.5 %copy-done = bf16[192,64,576]{2,1,0:T(8,128)(2,1)S(1)} copy-done((bf16[192,64,576]{2,1,0:T(8,128)(2,1)S(1)}, bf16[192,64,576]{2,1,0:T(8,128)(2,1)}, u32[]{:S(2)}) %copy-start) | copy-done | bytes 14155800
  5.5 0.0 copy-start.3
  5.5 1.0 %copy-done.3 = bf16[4,64,576]{2,1,0:T(8,128)(2,1)S(1)} copy-done((bf16[4,64,576]{2,1,0:T(8,128)(2,1)S(1)}, bf16[4,64,576]{2,1,0:T(8,128)(2,1)}, u32[]{:S(2)}) %copy-start.3) | copy-done | bytes 294936
  6.4 0.0 copy-start.7
  6.4 0.7 copy-done.7
  7.1 0.0 copy-start.1
  7.1 0.0 copy-start.2
  7.1 0.0 copy-start.4
  7.1 0.0 copy-start.5
  7.1 0.0 copy-start.6
  7.1 16.2 %attention.1.partial_hbm = bf16[16,16,640]{2,1,0:T(8,128)(2,1)S(1)} custom-call(s32[192]{0:T(256)S(1)} %copy-done.7, bf16[4,64,576]{2,1,0:T(8,128)(2,1)S(1)} %copy-done.3, bf16[192,64,576]{2,1,0:T(8,128)(2,1)S(1)} %copy-done), custom_call_target="tpu_custom_call" | custom-call | tf_op jit(solution)/shard_map/attention/pallas_call | solution.py:89
  23.3 0.0 copy-done.1
  23.3 0.0 copy-done.2
  23.4 0.0 copy-done.4
  23.4 0.0 copy-done.5
  23.4 0.0 copy-done.6
  23.4 46.0 %layer.1 = bf16[4,512]{1,0:T(4,128)(2,1)S(1)} custom-call(bf16[16,16,640]{2,1,0:T(8,128)(2,1)S(1)} %attention.1.partial_hbm, bf16[4,512,128]{2,1,0:T(8,128)(2,1)S(1)} %copy-done.2, bf16[512,7168]{1,0:T(8,128)(2,1)} %outw_hbm.1, f32[56,128]{1,0:T(8,128)S(1)} %bitcast.2, s32[4,8]{1,0:T(4,128)S(1)} %copy-done.5, f32[4,8]{1,0:T(4,128)S(1)} %copy-done.6, ...), custom_call_target="tpu_custom_call" | custom-call | tf_op jit(solution)/shard_map/layer/pallas_call | solution.py:368
  69.4 0.7 constant_dynamic-slice_fusion
Async XLA Ops:
  0.0 5.5 %copy-start = (bf16[192,64,576]{2,1,0:T(8,128)(2,1)S(1)}, bf16[192,64,576]{2,1,0:T(8,128)(2,1)}, u32[]{:S(2)}) copy-start(bf16[192,64,576]{2,1,0:T(8,128)(2,1)} %cache_ref.1) | copy-start | bytes 42467332
  5.5 1.0 %copy-start.3 = (bf16[4,64,576]{2,1,0:T(8,128)(2,1)S(1)}, bf16[4,64,576]{2,1,0:T(8,128)(2,1)}, u32[]{:S(2)}) copy-start(bf16[4,64,576]{2,1,0:T(8,128)(2,1)} %q_ref.1) | copy-start | bytes 884740
  6.4 0.7 copy-start.7
  7.1 16.2 %copy-start.1 = (bf16[2,7168,128]{2,1,0:T(8,128)(2,1)S(1)}, bf16[2,7168,128]{2,1,0:T(8,128)(2,1)}, u32[]{:S(2)}) copy-start(bf16[2,7168,128]{2,1,0:T(8,128)(2,1)} %gate_hbm.1) | copy-start | bytes 11010052
  7.1 16.2 %copy-start.2 = (bf16[4,512,128]{2,1,0:T(8,128)(2,1)S(1)}, bf16[4,512,128]{2,1,0:T(8,128)(2,1)}, u32[]{:S(2)}) copy-start(bf16[4,512,128]{2,1,0:T(8,128)(2,1)} %uv_hbm.1) | copy-start | bytes 1572868
  7.1 16.2 %copy-start.4 = (f32[7168]{0:T(1024)S(1)}, f32[7168]{0:T(1024)}, u32[]{:S(2)}) copy-start(f32[7168]{0:T(1024)} %param.16) | copy-start | bytes 86020
  7.1 16.2 %copy-start.5 = (s32[4,8]{1,0:T(4,128)S(1)}, s32[4,8]{1,0:T(4,128)}, u32[]{:S(2)}) copy-start(s32[4,8]{1,0:T(4,128)} %ids_ref.1) | copy-start | bytes 388
  7.1 16.2 %copy-start.6 = (f32[4,8]{1,0:T(4,128)S(1)}, f32[4,8]{1,0:T(4,128)}, u32[]{:S(2)}) copy-start(f32[4,8]{1,0:T(4,128)} %values_ref.1) | copy-start | bytes 388

commit v2 on v0

v2 whole, which is shorter than its diff:
```python
import functools
import jax
import jax.numpy as jnp
from jax import lax
from jax.experimental import pallas as pl
from jax.experimental.pallas import tpu as pltpu
from jax.sharding import PartitionSpec as P

SCORE_SCALE = 192.0 ** (-0.5)
LOG2E = 1.4426950408889634
EPSILON = 1e-06
MASKED = -1e30
FLOOR = -1e20
F32 = jnp.float32
BF16 = jnp.bfloat16
MESH = pl.DeviceIdType.MESH

NX = 4
PAGES = 192
STEP_PAGES = 32
LOAD_PAGES = 16
START_WEIGHTS = 3


def hops(steps):
    return sum(min(d, NX - d) for d in steps)


OFFSETS = sorted(
    [(z, x, y) for z in range(NX) for x in range(NX) for y in range(NX) if (z, x, y) != (0, 0, 0)],
    key=lambda d: -hops(d),
)
PLANE = [d[1:] for d in OFFSETS if d[0] == 0]
PAIRS = [(0, 0), (0, 1), (1, 0), (3, 0), (1, 1), (3, 1), (2, 0), (2, 1)]


def split_bf16(value, parts):
    out = []
    for _ in range(parts):
        piece = value.astype(BF16).astype(F32)
        out.append(piece)
        value = value - piece
    return out


def window_tile(e):
    return (e // 2) * 7 + (e % 2) * 3


def layer_kernel(
    queries_hbm, cache_hbm, owner_hbm, uv_hbm, outw_hbm, gain_hbm, ids_hbm, values_hbm, gate_hbm, up_hbm, down_hbm,
    out_ref,
    owner, queries, q_rows, cache, scores, peak_ref, total_ref, value_ref,
    uv, outw, gain, ids_ref, values_ref, gate, up, down,
    part_send, part_recv, term_send, term_recv, x_mine, x_buf,
    swap_send, swap_keep, swap_recv, back_send, back_recv,
    load_sem, cache_sem, s1, r1, s2, r2, s3, r3, s4, r4, s5, r5, s6, r6, s7, r7, s8, r8,
):
    a = lax.axis_index("attn")
    e = lax.axis_index("expert")
    z = a // 2
    core = a % 2
    ex = e // NX
    ey = e % NX
    odd = e % 2
    sibling = {"attn": z * 2 + (1 - core)}

    def plane_peer(x, y):
        return lax.rem(ex + x, NX) * NX + lax.rem(ey + y, NX)

    def z_peer(k):
        return lax.rem(z + k, NX)

    def device(k, x, y):
        return {"attn": z_peer(k) * 2 + core, "expert": plane_peer(x, y)}

    def remote(src, dst, send, recv, to):
        return pltpu.make_async_remote_copy(
            src_ref=src, dst_ref=dst, send_sem=send, recv_sem=recv, device_id=to, device_id_type=MESH
        )

    owner_load = pltpu.make_async_copy(owner_hbm, owner, load_sem.at[0])
    queries_load = pltpu.make_async_copy(queries_hbm, queries, load_sem.at[1])
    owner_load.start()
    queries_load.start()
    cache_loads = []
    for c in range(PAGES // LOAD_PAGES):
        at = pl.ds(c * LOAD_PAGES, LOAD_PAGES)
        cache_loads.append(pltpu.make_async_copy(cache_hbm.at[at], cache.at[at], cache_sem.at[c]))
        cache_loads[-1].start()
    loads = [
        pltpu.make_async_copy(src, dst, load_sem.at[n + 2])
        for n, (src, dst) in enumerate(
            [(uv_hbm, uv), (outw_hbm, outw), (gain_hbm, gain), (ids_hbm, ids_ref), (values_hbm, values_ref),
             (gate_hbm, gate), (up_hbm, up), (down_hbm, down)]
        )
    ]
    barrier = pltpu.get_barrier_semaphore()
    for offset in OFFSETS:
        pl.semaphore_signal(barrier, inc=1, device_id=device(*offset), device_id_type=MESH)
    pl.semaphore_signal(barrier, inc=1, device_id=sibling, device_id_type=MESH)

    owner_load.wait()
    queries_load.wait()
    rows = 256
    i = lax.broadcasted_iota(jnp.int32, (rows, rows), 0)
    j = lax.broadcasted_iota(jnp.int32, (rows, rows), 1)
    order = (j == (i % 4) * 64 + i // 4).astype(F32).astype(BF16)
    q_rows[...] = jnp.dot(order, queries[...].reshape(rows, 576), preferred_element_type=F32).astype(BF16)
    lane8 = lax.broadcasted_iota(jnp.int32, (8, 128), 1)
    request = lax.broadcasted_iota(jnp.int32, (8, 128), 0) % 4
    tokens = STEP_PAGES * 64
    steps = PAGES // STEP_PAGES
    per = STEP_PAGES // LOAD_PAGES
    peak_ref[...] = jnp.full((rows, 128), FLOOR, F32)
    for c in range(steps):
        for load in cache_loads[c * per : (c + 1) * per]:
            load.wait()
        if c == START_WEIGHTS:
            for load in loads:
                load.start()
        keys = cache[c * STEP_PAGES : (c + 1) * STEP_PAGES].reshape(tokens, 576)
        raw = lax.dot_general(q_rows[...], keys, (((1,), (1,)), ((), ())), preferred_element_type=F32)
        peak = peak_ref[...]
        for pair in range(STEP_PAGES // 2):
            first = owner[c * STEP_PAGES + 2 * pair]
            second = owner[c * STEP_PAGES + 2 * pair + 1]
            bias = jnp.where(jnp.where(lane8 < 64, first, second) == request, 0.0, MASKED)
            tile = raw[:, 128 * pair : 128 * pair + 128].reshape(32, 8, 128) * (SCORE_SCALE * LOG2E) + bias[None]
            tile = tile.reshape(rows, 128)
            scores[c, :, 128 * pair : 128 * pair + 128] = tile
            peak = jnp.maximum(peak, tile)
        peak_ref[...] = peak
    peak = jnp.max(peak_ref[...], axis=1, keepdims=True)
    peak_ref[...] = jnp.broadcast_to(peak, (rows, 128))
    total_ref[...] = jnp.zeros((rows, 128), F32)
    value_ref[...] = jnp.zeros((rows, 512), F32)

    def weigh(c, carry):
        peak = peak_ref[...]
        total = total_ref[...]
        probs = []
        for pair in range(STEP_PAGES // 2):
            prob = jnp.exp2(scores[c, :, 128 * pair : 128 * pair + 128] - peak)
            total = total + prob
            probs.append(prob.astype(BF16))
        total_ref[...] = total
        values = cache[pl.ds(c * STEP_PAGES, STEP_PAGES), :, :512].reshape(tokens, 512)
        value_ref[...] += jnp.dot(jnp.concatenate(probs, axis=1), values, preferred_element_type=F32)
        return carry

    lax.fori_loop(0, steps, weigh, 0)
    total = jnp.sum(total_ref[...], axis=1, keepdims=True)
    safe = jnp.where(total > 0.0, total, 1.0)
    lse = jnp.where(total > 0.0, peak_ref[...] + jnp.log2(safe), FLOOR)
    wide = lax.broadcasted_iota(jnp.int32, (rows, 128), 1)
    coded = jnp.zeros((rows, 128), F32)
    for at, piece in enumerate(split_bf16(lse, 3)):
        coded = jnp.where(wide == at, piece, coded)
    part_send[:, :, :512] = (value_ref[...] / safe).astype(BF16).reshape(16, 16, 512)
    part_send[:, :, 512:] = coded.astype(BF16).reshape(16, 16, 128)

    pl.semaphore_wait(barrier, len(OFFSETS) + 1)
    sends = []
    first = []
    for k, offset in enumerate(PLANE):
        to = plane_peer(*offset)
        first.append(remote(part_send.at[to], part_recv.at[k], s1.at[k], r1.at[k], {"expert": to}))
        first[-1].start()
    sends += first

    for load in loads[:5]:
        load.wait()
    lane = lax.broadcasted_iota(jnp.int32, (16, 128), 1)
    row = lax.broadcasted_iota(jnp.int32, (16, 128), 0)
    spot = lane % 64
    ids = jnp.concatenate([ids_ref[...]] * 4, axis=0)
    shares = jnp.concatenate([values_ref[...]] * 4, axis=0)
    expert_at = jnp.where(spot < 32, spot - 16, spot - 32)
    expert_at = jnp.where((spot >= 16) & (spot < 48), expert_at, -1)
    routing = jnp.zeros((16, 128), F32)
    for k in range(8):
        routing += jnp.where(ids[:, k : k + 1] == expert_at, shares[:, k : k + 1], 0.0)
    high, low = split_bf16(routing, 2)
    coded = jnp.where(spot < 32, high, low)
    side = (row // 4 == 3 * (1 - odd)) & (lane // 64 == 1 - odd)

    for copy in first:
        copy.wait_recv()

    def part(s):
        return part_send[e] if s == len(PLANE) else part_recv[s]

    lse = [jnp.sum(part(s)[:, 512:].astype(F32), axis=1, keepdims=True) for s in range(16)]
    peak = functools.reduce(jnp.maximum, lse)
    total = jnp.zeros_like(peak)
    summed = jnp.zeros((16, 512), F32)
    for s in range(16):
        weight = jnp.exp2(lse[s] - peak)
        total += weight
        summed += weight * part(s)[:, :512].astype(F32)
    attended = (summed / total).astype(BF16)
    mixed = []
    for h in range(4):
        mapped = jnp.dot(attended, uv[h], preferred_element_type=F32)
        mixed.append(jnp.concatenate([mapped[4 * h : 4 * h + 4]] * 4, axis=0))
    mixed = jnp.concatenate(mixed, axis=1).astype(BF16)

    def terms(to):
        start = pl.multiple_of(window_tile(to) * 128, 128)
        wide = jnp.dot(mixed, outw[:, pl.ds(start, 512)], preferred_element_type=F32)
        folded = wide[:, :128]
        for j in range(1, 4):
            folded = jnp.where(row // 4 == j, wide[:, 128 * j : 128 * j + 128], folded)
        return folded

    second = []
    for k, offset in enumerate(PLANE):
        to = plane_peer(*offset)
        term_send[k] = terms(to).astype(BF16)
        second.append(remote(term_send.at[k], term_recv.at[k], s2.at[k], r2.at[k], {"expert": to}))
        second[-1].start()
    sends += second
    attn_out = terms(e)
    for k, copy in enumerate(second):
        copy.wait_recv()
        attn_out += term_recv[k].astype(F32)

    gains = gain[pl.ds(window_tile(e), 4), :]
    gains = jnp.concatenate([jnp.broadcast_to(gains[j : j + 1], (4, 128)) for j in range(4)], axis=0)
    squares = jnp.sum(jnp.where(side, 0.0, attn_out * attn_out), axis=1, keepdims=True)
    squares = squares[0:4] + squares[4:8] + squares[8:12] + squares[12:16]
    squares = jnp.broadcast_to(jnp.concatenate([squares] * 4, axis=0), (16, 128))
    high, low = split_bf16(squares, 2)
    coded = jnp.where(spot == 0, high, jnp.where(spot == 1, low, coded))
    x_mine[...] = jnp.where(side, coded, attn_out * gains).astype(BF16)
    x_buf[e, core, z] = x_mine[...]
    for k, x, y in OFFSETS:
        to = device(k, x, y)
        if (x, y) == (0, 0):
            copy = remote(x_mine, x_buf.at[e, core, z], s3.at[k - 1], r3.at[z], to)
            sends.append(copy)
        else:
            copy = remote(x_mine, x_buf.at[e, core, z], s4.at[PLANE.index((x, y))], r4.at[e], to)
        copy.start()
    for x, yy in PAIRS:
        for half in range(2):
            source = lax.rem(ex + x, NX) * NX + lax.rem(ey // 2 + yy, 2) * 2 + (odd + half) % 2
            if (x, yy, half) == (0, 0, 0):
                for k in range(1, NX):
                    there = z_peer(k)
                    remote(x_mine, x_buf.at[e, core, there], s3.at[0], r3.at[there], sibling).wait_recv()
            else:
                block = x_buf.at[source, core]
                remote(block, block, s4.at[0], r4.at[source], sibling).wait_recv()
            block = x_buf.at[source, core]
            copy = remote(block, block, s5.at[source], r5.at[source], sibling)
            copy.start()
            sends.append(copy)

    for load in loads[5:]:
        load.wait()
    products = [jnp.zeros((32, 256), F32) for _ in range(2)]
    squares = jnp.zeros((32, 1), F32)
    lane32 = lax.broadcasted_iota(jnp.int32, (32, 128), 1)
    i = lax.broadcasted_iota(jnp.int32, (128, 128), 0)
    j = lax.broadcasted_iota(jnp.int32, (128, 128), 1)
    unfold = (j == (i // 4 % 8) * 16 + (i // 32) * 4 + i % 4).astype(F32).astype(BF16)
    for step, (x, yy) in enumerate(PAIRS):
        pair = lax.rem(ex + x, NX) * 2 + lax.rem(ey // 2 + yy, 2)
        for half in range(2):
            source = pair * 2 + half
            block = x_buf.at[source, 1 - core]
            remote(block, block, s5.at[source], r5.at[source], sibling).wait_recv()
        both = jnp.concatenate([x_buf[pair * 2 + half].reshape(128, 128) for half in range(2)], axis=1)
        both = jnp.dot(unfold, both, preferred_element_type=F32)
        even = [both[32 * n : 32 * n + 32, :128] for n in range(4)]
        odds = [both[32 * n : 32 * n + 32, 128:] for n in range(4)]
        middle = jnp.where(lane32 < 64, even[3], odds[0])
        extra = jnp.where(lane32 < 64, odds[0], even[3])
        squares += jnp.sum(jnp.where(lane32 % 64 < 2, extra, 0.0), axis=1, keepdims=True)
        rows_in = jnp.concatenate(even[:3] + [middle] + odds[1:], axis=1).astype(BF16)
        at = pl.ds(pl.multiple_of(pair * 896, 128), 896)
        for n in range(2):
            weights = jnp.concatenate([gate[n, at, :], up[n, at, :]], axis=1)
            products[n] += jnp.dot(rows_in, weights, preferred_element_type=F32)
        if step == 0:
            share = []
            for n in range(2):
                number = (1 - odd) * 64 + 2 * a + n
                chosen = (lane32 == number + 16) | (lane32 == number + 32)
                share.append(jnp.sum(jnp.where(chosen, extra, 0.0), axis=1, keepdims=True))
    scale = lax.rsqrt(squares / 7168.0 + EPSILON)
    hidden = []
    for n in range(2):
        g = products[n][:, :128] * scale
        u = products[n][:, 128:] * scale
        hidden.append(g / (1.0 + jnp.exp(-g)) * u * share[n])
    hidden = jnp.concatenate(hidden, axis=1).astype(BF16)
    i = lax.broadcasted_iota(jnp.int32, (128, 32), 0)
    j = lax.broadcasted_iota(jnp.int32, (128, 32), 1)
    repeat = (j == i // 16 * 4 + i % 4).astype(F32).astype(BF16)
    hidden = jnp.dot(repeat, hidden, preferred_element_type=F32).astype(BF16)

    row128 = lax.broadcasted_iota(jnp.int32, (128, 128), 0)
    targets = [plane_peer(*offset) for offset in PLANE] + [e]
    swap = []
    for k, to in enumerate(targets):
        start = pl.multiple_of(window_tile(to) * 128, 128)
        wide = jnp.dot(hidden, down[:, pl.ds(start, 512)], preferred_element_type=F32)
        folded = wide[:, :128]
        for j in range(1, 4):
            folded = jnp.where(row128 // 4 % 4 == j, wide[:, 128 * j : 128 * j + 128], folded)
        top, bottom = folded[:64], folded[64:]
        swap_keep[k] = jnp.where(core == 0, top, bottom)
        swap_send[k] = jnp.where(core == 0, bottom, top).astype(BF16)
        swap.append(remote(swap_send.at[k], swap_recv.at[k], s6.at[k], r6.at[k], sibling))
        swap[-1].start()
    sends += swap

    last = []
    for k, to in enumerate(targets):
        swap[k].wait_recv()
        both = swap_keep[k] + swap_recv[k].astype(F32)
        back_send[k] = both.astype(BF16).reshape(NX, 16, 128)
        for n in range(NX):
            there = z_peer(n)
            where = {"attn": there * 2 + core, "expert": to}
            if k < len(PLANE):
                remote(back_send.at[k, there], back_recv.at[k, n], s7.at[k], r7.at[k], where).start()
            elif n > 0:
                last.append(remote(back_send.at[k, there], back_recv.at[k, n], s8.at[n - 1], r8.at[n - 1], where))
                last[-1].start()
    sends += last
    result = attn_out + back_send[len(PLANE), z].astype(F32)
    for n, copy in enumerate(last):
        copy.wait_recv()
        result += back_recv[len(PLANE), n + 1].astype(F32)
    for k in range(len(PLANE)):
        remote(back_recv.at[k], back_recv.at[k], s7.at[k], r7.at[k], sibling).wait_recv()
        for n in range(NX):
            result += back_recv[k, n].astype(F32)
    out_ref[...] = jnp.concatenate([result[4 * j : 4 * j + 4] for j in range(4)], axis=1).astype(BF16)
    for copy in sends:
        copy.wait_send()
    for k in range(len(PLANE)):
        remote(back_send.at[k], back_recv.at[k], s4.at[k], r7.at[k], sibling).wait_send()
        remote(back_send.at[k], back_recv.at[k], s7.at[k], r7.at[k], sibling).wait_send()


def layer(queries, cache, owner, uv, outw, gain, ids, values, gate, up, down):
    dma = pltpu.SemaphoreType.DMA
    hbm = pl.BlockSpec(memory_space=pl.ANY)
    steps = PAGES // STEP_PAGES
    return pl.pallas_call(
        layer_kernel,
        out_shape=jax.ShapeDtypeStruct((4, 512), BF16),
        in_specs=[hbm] * 11,
        out_specs=pl.BlockSpec(memory_space=pltpu.VMEM),
        scratch_shapes=[
            pltpu.SMEM(owner.shape, jnp.int32),
            pltpu.VMEM(queries.shape, BF16),
            pltpu.VMEM((256, 576), BF16),
            pltpu.VMEM(cache.shape, BF16),
            pltpu.VMEM((steps, 256, STEP_PAGES * 64), F32),
            pltpu.VMEM((256, 128), F32),
            pltpu.VMEM((256, 128), F32),
            pltpu.VMEM((256, 512), F32),
            pltpu.VMEM(uv.shape, BF16),
            pltpu.VMEM(outw.shape, BF16),
            pltpu.VMEM(gain.shape, F32),
            pltpu.VMEM(ids.shape, jnp.int32),
            pltpu.VMEM(values.shape, F32),
            pltpu.VMEM(gate.shape, BF16),
            pltpu.VMEM(up.shape, BF16),
            pltpu.VMEM(down.shape, BF16),
            pltpu.VMEM((16, 16, 640), BF16),
            pltpu.VMEM((15, 16, 640), BF16),
            pltpu.VMEM((15, 16, 128), BF16),
            pltpu.VMEM((15, 16, 128), BF16),
            pltpu.VMEM((16, 128), BF16),
            pltpu.VMEM((16, 2, NX, 16, 128), BF16),
            pltpu.VMEM((16, 64, 128), BF16),
            pltpu.VMEM((16, 64, 128), F32),
            pltpu.VMEM((16, 64, 128), BF16),
            pltpu.VMEM((16, NX, 16, 128), BF16),
            pltpu.VMEM((16, NX, 16, 128), BF16),
            dma((10,)), dma((PAGES // LOAD_PAGES,)),
            dma((15,)), dma((15,)),
            dma((15,)), dma((15,)),
            dma((3,)), dma((4,)),
            dma((15,)), dma((16,)),
            dma((16,)), dma((16,)),
            dma((16,)), dma((16,)),
            dma((15,)), dma((15,)),
            dma((3,)), dma((3,)),
        ],
        compiler_params=pltpu.CompilerParams(
            collective_id=0, has_side_effects=True, vmem_limit_bytes=60 << 20
        ),
        name="layer",
    )(queries, cache, owner, uv, outw, gain, ids, values, gate, up, down)


def on_device(
    queries, cache, owner, uv_weight, out_weight, norm_gain, expert_ids, gate_values,
    gate_weight, up_weight, down_weight,
):
    wide = layer(
        queries, cache, owner, uv_weight, out_weight, norm_gain.reshape(56, 128), expert_ids, gate_values,
        gate_weight, up_weight, down_weight.reshape(256, 7168),
    )
    start = (lax.axis_index("expert") % 2) * 64
    return lax.dynamic_slice_in_dim(wide, start, 448, 1)


def solution(mesh):
    placed = (
        P("attn", None, None),
        P(("attn", "expert"), None, None),
        P(("attn", "expert")),
        P("expert", None, None),
        P("expert", None),
        P(),
        P("attn", None),
        P("attn", None),
        P("attn", None, "expert"),
        P("attn", None, "expert"),
        P("attn", "expert", None),
    )
    return jax.shard_map(
        on_device, mesh=mesh, in_specs=placed, out_specs=P("attn", "expert"), check_vma=False
    )
```

time: 385 us -> 56.8 us (0.15)
  waiting for transfers between devices: 167 us -> 0 us
  matrix products: 73.9 us -> 0 us
  local copies, waits for them, and re-layouts: 71.5 us -> 1.36 us
  Pallas kernels: 0 us -> 55.3 us
  starting transfers between devices: 27.8 us -> 0 us
  blocking collectives: 20.8 us -> 0 us
  between operations: 13.6 us -> 0.01 us
  other arithmetic: 9.93 us -> 0 us
    psum x1 -> x0, waiting for transfers between devices: 81.8 us -> none  [on_device(): attn_out = lax.psum(partial_out, 'expert')]
    dot_general x10 -> x0, matrix products: 73.9 us -> none  [the longest x1 28.2 us: local_attention(): jnp.dot(member_float.T, page_sum.reshape(pool_size, -1), precision=HIGHEST)]
    unnamed x3 -> x0, waiting for transfers between devices: 71.8 us -> none
    pallas_call x0 -> x1, Pallas kernels: none -> 55.3 us  [layer(): pl.pallas_call(layer_kernel, out_shape=jax.ShapeDtypeStruct((4, 512), BF1...]
    unnamed x16 -> x0, local copies, waits for them, and re-layouts: 45.4 us -> none
    all_to_all x4 -> x0, starting transfers between devices: 27.5 us -> none  [the longest x1 7.39 us: on_device(): lax.all_to_all(totals[None], 'expert', split_axis=2, concat_axis=0, tiled...]
    all_to_all x1 -> x0, blocking collectives: 20.8 us -> none  [round_trip(): lax.all_to_all(slot_block, 'attn', split_axis=0, concat_axis=0, tiled=True)]
    all_to_all x4 -> x0, waiting for transfers between devices: 12.9 us -> none  [the longest x1 7.74 us: on_device(): lax.all_to_all(summed[None], 'expert', split_axis=2, concat_axis=0, tiled...]
  transfers between devices with their start and end apart: 6 -> 0, of which waited for: 4 -> 0; matrix products, arithmetic and copies ran while one was open for 13% -> 0% of each run, Pallas kernels for 0% -> 0%
where the time goes in v2:
time: 56.8 us; the launch traced here: 56.7 us
  Pallas kernels  55.3 us (97%)
  local copies, waits for them, and re-layouts  1.36 us (2%)
    pallas_call x1, Pallas kernels, layer(): pl.pallas_call(layer_kernel, out_shape=jax.ShapeDtypeStruct((4, 512), BF1...  55.3 us
    dynamic_slice x1, local copies, waits for them, and re-layouts, on_device(): return lax.dynamic_slice_in_dim(wide, start, 448, 1)  1.36 us

profile of v2, /device:TPU:1, one launch (start us, length us, event | category | flops | bytes accessed | tf_op | source)
XLA Modules:
  0.0 56.7 jit_solution(6999477055935481087)
XLA Ops:
  0.0 55.3 %layer.1 = bf16[4,512]{1,0:T(4,128)(2,1)} custom-call(bf16[4,64,576]{2,1,0:T(8,128)(2,1)} %queries_hbm.1, bf16[192,64,576]{2,1,0:T(8,128)(2,1)} %cache_hbm.1, s32[192]{0:T(256)} %owner_hbm.1, bf16[4,512,128]{2,1,0:T(8,128)(2,1)} %uv_hbm.1, bf16[512,7168]{1,0:T(8,128)(2,1)} %outw_hbm.1, f32[56,128]{1,0:T(8,128)} %bitcast.3, s32[4,8]{1,0:T(4,128)} %ids_hbm.1, ...), custom_call_target="tpu_custom_call" | custom-call | tf_op jit(solution)/shard_map/layer/pallas_call | solution.py:355
  55.4 1.4 %constant_dynamic-slice_fusion = bf16[4,448]{1,0:T(4,128)(2,1)} fusion(bf16[4,512]{1,0:T(4,128)(2,1)} %layer.1, s32[]{:T(128)S(6)} %select_n.11), kind=kLoop, calls=%fused_computation | loop fusion | bytes 7172 | tf_op jit(solution)/shard_map/dynamic_slice | solution.py:414

commit v3 on v2

--- a/solution.py
+++ b/solution.py
@@ -18,8 +18,8 @@
 NX = 4
 PAGES = 192
 STEP_PAGES = 32
-LOAD_PAGES = 16
-START_WEIGHTS = 3
+LOAD_PAGES = 32
+START_WEIGHTS = 0
 
 
 def hops(steps):
@@ -31,6 +31,8 @@
     key=lambda d: -hops(d),
 )
 PLANE = [d[1:] for d in OFFSETS if d[0] == 0]
+LAG = 8
+AHEAD = 2
 PAIRS = [(0, 0), (0, 1), (1, 0), (3, 0), (1, 1), (3, 1), (2, 0), (2, 1)]
 
 
@@ -50,7 +52,7 @@
 def layer_kernel(
     queries_hbm, cache_hbm, owner_hbm, uv_hbm, outw_hbm, gain_hbm, ids_hbm, values_hbm, gate_hbm, up_hbm, down_hbm,
     out_ref,
-    owner, queries, q_rows, cache, scores, peak_ref, total_ref, value_ref,
+    owner, queries, q_rows, cache, scores_even, scores_odd, top_even, top_odd, peak_ref, total_ref, value_ref,
     uv, outw, gain, ids_ref, values_ref, gate, up, down,
     part_send, part_recv, term_send, term_recv, x_mine, x_buf,
     swap_send, swap_keep, swap_recv, back_send, back_recv,
@@ -96,9 +98,13 @@
         )
     ]
     barrier = pltpu.get_barrier_semaphore()
-    for offset in OFFSETS:
-        pl.semaphore_signal(barrier, inc=1, device_id=device(*offset), device_id_type=MESH)
+
+    def greet(offsets):
+        for offset in offsets:
+            pl.semaphore_signal(barrier, inc=1, device_id=device(*offset), device_id_type=MESH)
+
     pl.semaphore_signal(barrier, inc=1, device_id=sibling, device_id_type=MESH)
+    greet(OFFSETS)
 
     owner_load.wait()
     queries_load.wait()
@@ -113,7 +119,12 @@
     steps = PAGES // STEP_PAGES
     per = STEP_PAGES // LOAD_PAGES
     peak_ref[...] = jnp.full((rows, 128), FLOOR, F32)
-    for c in range(steps):
+    total_ref[...] = jnp.zeros((rows, 128), F32)
+    value_ref[...] = jnp.zeros((rows, 512), F32)
+    scores = (scores_even, scores_odd)
+    tops = (top_even, top_odd)
+
+    def score(c):
         for load in cache_loads[c * per : (c + 1) * per]:
             load.wait()
         if c == START_WEIGHTS:
@@ -121,35 +132,39 @@
                 load.start()
         keys = cache[c * STEP_PAGES : (c + 1) * STEP_PAGES].reshape(tokens, 576)
         raw = lax.dot_general(q_rows[...], keys, (((1,), (1,)), ((), ())), preferred_element_type=F32)
-        peak = peak_ref[...]
+        top = None
         for pair in range(STEP_PAGES // 2):
             first = owner[c * STEP_PAGES + 2 * pair]
             second = owner[c * STEP_PAGES + 2 * pair + 1]
             bias = jnp.where(jnp.where(lane8 < 64, first, second) == request, 0.0, MASKED)
             tile = raw[:, 128 * pair : 128 * pair + 128].reshape(32, 8, 128) * (SCORE_SCALE * LOG2E) + bias[None]
             tile = tile.reshape(rows, 128)
-            scores[c, :, 128 * pair : 128 * pair + 128] = tile
-            peak = jnp.maximum(peak, tile)
+            scores[c % 2][:, 128 * pair : 128 * pair + 128] = tile
+            top = tile if top is None else jnp.maximum(top, tile)
+        tops[c % 2][...] = top
+
+    def weigh(c):
+        old = peak_ref[...]
+        top = jnp.max(tops[c % 2][...], axis=1, keepdims=True)
+        peak = jnp.maximum(old, jnp.broadcast_to(top, (rows, 128)))
+        alpha = jnp.exp2(old - peak)
         peak_ref[...] = peak
-    peak = jnp.max(peak_ref[...], axis=1, keepdims=True)
-    peak_ref[...] = jnp.broadcast_to(peak, (rows, 128))
-    total_ref[...] = jnp.zeros((rows, 128), F32)
-    value_ref[...] = jnp.zeros((rows, 512), F32)
-
-    def weigh(c, carry):
-        peak = peak_ref[...]
-        total = total_ref[...]
+        total = total_ref[...] * alpha
         probs = []
         for pair in range(STEP_PAGES // 2):
-            prob = jnp.exp2(scores[c, :, 128 * pair : 128 * pair + 128] - peak)
+            prob = jnp.exp2(scores[c % 2][:, 128 * pair : 128 * pair + 128] - peak)
             total = total + prob
             probs.append(prob.astype(BF16))
         total_ref[...] = total
-        values = cache[pl.ds(c * STEP_PAGES, STEP_PAGES), :, :512].reshape(tokens, 512)
-        value_ref[...] += jnp.dot(jnp.concatenate(probs, axis=1), values, preferred_element_type=F32)
-        return carry
-
-    lax.fori_loop(0, steps, weigh, 0)
+        values = cache[c * STEP_PAGES : (c + 1) * STEP_PAGES, :, :512].reshape(tokens, 512)
+        added = jnp.dot(jnp.concatenate(probs, axis=1), values, preferred_element_type=F32)
+        value_ref[...] = value_ref[...] * jnp.concatenate([alpha] * 4, axis=1) + added
+
+    score(0)
+    for c in range(steps):
+        if c + 1 < steps:
+            score(c + 1)
+        weigh(c)
     total = jnp.sum(total_ref[...], axis=1, keepdims=True)
     safe = jnp.where(total > 0.0, total, 1.0)
     lse = jnp.where(total > 0.0, peak_ref[...] + jnp.log2(safe), FLOOR)
@@ -162,12 +177,9 @@
 
     pl.semaphore_wait(barrier, len(OFFSETS) + 1)
     sends = []
-    first = []
     for k, offset in enumerate(PLANE):
         to = plane_peer(*offset)
-        first.append(remote(part_send.at[to], part_recv.at[k], s1.at[k], r1.at[k], {"expert": to}))
-        first[-1].start()
-    sends += first
+        remote(part_send.at[to], part_recv.at[k], s1, r1, {"expert": to}).start()
 
     for load in loads[:5]:
         load.wait()
@@ -185,8 +197,7 @@
     coded = jnp.where(spot < 32, high, low)
     side = (row // 4 == 3 * (1 - odd)) & (lane // 64 == 1 - odd)
 
-    for copy in first:
-        copy.wait_recv()
+    remote(part_recv, part_recv, s1, r1, sibling).wait_recv()
 
     def part(s):
         return part_send[e] if s == len(PLANE) else part_recv[s]
@@ -214,16 +225,13 @@
             folded = jnp.where(row // 4 == j, wide[:, 128 * j : 128 * j + 128], folded)
         return folded
 
-    second = []
     for k, offset in enumerate(PLANE):
         to = plane_peer(*offset)
         term_send[k] = terms(to).astype(BF16)
-        second.append(remote(term_send.at[k], term_recv.at[k], s2.at[k], r2.at[k], {"expert": to}))
-        second[-1].start()
-    sends += second
+        remote(term_send.at[k], term_recv.at[k], s2, r2, {"expert": to}).start()
     attn_out = terms(e)
-    for k, copy in enumerate(second):
-        copy.wait_recv()
+    remote(term_recv, term_recv, s2, r2, sibling).wait_recv()
+    for k in range(len(PLANE)):
         attn_out += term_recv[k].astype(F32)
 
     gains = gain[pl.ds(window_tile(e), 4), :]
@@ -241,9 +249,10 @@
             copy = remote(x_mine, x_buf.at[e, core, z], s3.at[k - 1], r3.at[z], to)
             sends.append(copy)
         else:
-            copy = remote(x_mine, x_buf.at[e, core, z], s4.at[PLANE.index((x, y))], r4.at[e], to)
+            copy = remote(x_mine, x_buf.at[e, core, z], s4, r4.at[e], to)
         copy.start()
-    for x, yy in PAIRS:
+
+    def pass_on(x, yy):
         for half in range(2):
             source = lax.rem(ex + x, NX) * NX + lax.rem(ey // 2 + yy, 2) * 2 + (odd + half) % 2
             if (x, yy, half) == (0, 0, 0):
@@ -252,11 +261,9 @@
                     remote(x_mine, x_buf.at[e, core, there], s3.at[0], r3.at[there], sibling).wait_recv()
             else:
                 block = x_buf.at[source, core]
-                remote(block, block, s4.at[0], r4.at[source], sibling).wait_recv()
+                remote(block, block, s4, r4.at[source], sibling).wait_recv()
             block = x_buf.at[source, core]
-            copy = remote(block, block, s5.at[source], r5.at[source], sibling)
-            copy.start()
-            sends.append(copy)
+            remote(block, block, s5, r5.at[source], sibling).start()
 
     for load in loads[5:]:
         load.wait()
@@ -266,12 +273,16 @@
     i = lax.broadcasted_iota(jnp.int32, (128, 128), 0)
     j = lax.broadcasted_iota(jnp.int32, (128, 128), 1)
     unfold = (j == (i // 4 % 8) * 16 + (i // 32) * 4 + i % 4).astype(F32).astype(BF16)
+    for ahead in PAIRS[:AHEAD]:
+        pass_on(*ahead)
     for step, (x, yy) in enumerate(PAIRS):
+        if step + AHEAD < len(PAIRS):
+            pass_on(*PAIRS[step + AHEAD])
         pair = lax.rem(ex + x, NX) * 2 + lax.rem(ey // 2 + yy, 2)
         for half in range(2):
             source = pair * 2 + half
             block = x_buf.at[source, 1 - core]
-            remote(block, block, s5.at[source], r5.at[source], sibling).wait_recv()
+            remote(block, block, s5, r5.at[source], sibling).wait_recv()
         both = jnp.concatenate([x_buf[pair * 2 + half].reshape(128, 128) for half in range(2)], axis=1)
         both = jnp.dot(unfold, both, preferred_element_type=F32)
         even = [both[32 * n : 32 * n + 32, :128] for n in range(4)]
@@ -305,7 +316,9 @@
     row128 = lax.broadcasted_iota(jnp.int32, (128, 128), 0)
     targets = [plane_peer(*offset) for offset in PLANE] + [e]
     swap = []
-    for k, to in enumerate(targets):
+    last = []
+
+    def produce(k, to):
         start = pl.multiple_of(window_tile(to) * 128, 128)
         wide = jnp.dot(hidden, down[:, pl.ds(start, 512)], preferred_element_type=F32)
         folded = wide[:, :128]
@@ -314,47 +327,56 @@
         top, bottom = folded[:64], folded[64:]
         swap_keep[k] = jnp.where(core == 0, top, bottom)
         swap_send[k] = jnp.where(core == 0, bottom, top).astype(BF16)
-        swap.append(remote(swap_send.at[k], swap_recv.at[k], s6.at[k], r6.at[k], sibling))
+        swap.append(remote(swap_send.at[k], swap_recv.at[k], s6, r6.at[k], sibling))
         swap[-1].start()
-    sends += swap
-
-    last = []
-    for k, to in enumerate(targets):
+
+    def give_back(k, to):
         swap[k].wait_recv()
         both = swap_keep[k] + swap_recv[k].astype(F32)
         back_send[k] = both.astype(BF16).reshape(NX, 16, 128)
-        for n in range(NX):
+        for n in (2, 1, 3, 0):
             there = z_peer(n)
             where = {"attn": there * 2 + core, "expert": to}
             if k < len(PLANE):
-                remote(back_send.at[k, there], back_recv.at[k, n], s7.at[k], r7.at[k], where).start()
+                remote(back_send.at[k, there], back_recv.at[k, n], s7, r7, where).start()
             elif n > 0:
                 last.append(remote(back_send.at[k, there], back_recv.at[k, n], s8.at[n - 1], r8.at[n - 1], where))
                 last[-1].start()
+
+    for k, to in enumerate(targets):
+        produce(k, to)
+        if k >= LAG:
+            give_back(k - LAG, targets[k - LAG])
+    for k in range(len(targets) - LAG, len(targets)):
+        give_back(k, targets[k])
     sends += last
     result = attn_out + back_send[len(PLANE), z].astype(F32)
-    for n, copy in enumerate(last):
-        copy.wait_recv()
-        result += back_recv[len(PLANE), n + 1].astype(F32)
+    for n in (2, 1, 3):
+        remote(x_mine, back_recv.at[len(PLANE), n], s8.at[n - 1], r8.at[n - 1], sibling).wait_recv()
+        result += back_recv[len(PLANE), n].astype(F32)
+    most = pl.ds(0, len(PLANE))
+    remote(back_recv.at[most], back_recv.at[most], s7, r7, sibling).wait_recv()
     for k in range(len(PLANE)):
-        remote(back_recv.at[k], back_recv.at[k], s7.at[k], r7.at[k], sibling).wait_recv()
         for n in range(NX):
             result += back_recv[k, n].astype(F32)
-    out_ref[...] = jnp.concatenate([result[4 * j : 4 * j + 4] for j in range(4)], axis=1).astype(BF16)
+    wide = jnp.concatenate([result[4 * j : 4 * j + 4] for j in range(4)], axis=1)
+    out_ref[...] = jnp.where(odd == 1, wide[:, 64:], wide[:, :448]).astype(BF16)
     for copy in sends:
         copy.wait_send()
-    for k in range(len(PLANE)):
-        remote(back_send.at[k], back_recv.at[k], s4.at[k], r7.at[k], sibling).wait_send()
-        remote(back_send.at[k], back_recv.at[k], s7.at[k], r7.at[k], sibling).wait_send()
+    remote(part_recv, part_recv, s1, r1, sibling).wait_send()
+    remote(term_recv, term_recv, s2, r2, sibling).wait_send()
+    remote(back_send.at[most], back_recv.at[most], s4, r7, sibling).wait_send()
+    remote(swap_send, swap_recv, s5, r7, sibling).wait_send()
+    remote(swap_send, swap_recv, s6, r7, sibling).wait_send()
+    remote(back_send.at[most], back_recv.at[most], s7, r7, sibling).wait_send()
 
 
 def layer(queries, cache, owner, uv, outw, gain, ids, values, gate, up, down):
     dma = pltpu.SemaphoreType.DMA
     hbm = pl.BlockSpec(memory_space=pl.ANY)
-    steps = PAGES // STEP_PAGES
     return pl.pallas_call(
         layer_kernel,
-        out_shape=jax.ShapeDtypeStruct((4, 512), BF16),
+        out_shape=jax.ShapeDtypeStruct((4, 448), BF16),
         in_specs=[hbm] * 11,
         out_specs=pl.BlockSpec(memory_space=pltpu.VMEM),
         scratch_shapes=[
@@ -362,7 +384,10 @@
             pltpu.VMEM(queries.shape, BF16),
             pltpu.VMEM((256, 576), BF16),
             pltpu.VMEM(cache.shape, BF16),
-            pltpu.VMEM((steps, 256, STEP_PAGES * 64), F32),
+            pltpu.VMEM((256, STEP_PAGES * 64), F32),
+            pltpu.VMEM((256, STEP_PAGES * 64), F32),
+            pltpu.VMEM((256, 128), F32),
+            pltpu.VMEM((256, 128), F32),
             pltpu.VMEM((256, 128), F32),
             pltpu.VMEM((256, 128), F32),
             pltpu.VMEM((256, 512), F32),
@@ -386,13 +411,13 @@
             pltpu.VMEM((16, NX, 16, 128), BF16),
             pltpu.VMEM((16, NX, 16, 128), BF16),
             dma((10,)), dma((PAGES // LOAD_PAGES,)),
-            dma((15,)), dma((15,)),
-            dma((15,)), dma((15,)),
+            dma, dma,
+            dma, dma,
             dma((3,)), dma((4,)),
-            dma((15,)), dma((16,)),
-            dma((16,)), dma((16,)),
-            dma((16,)), dma((16,)),
-            dma((15,)), dma((15,)),
+            dma, dma((16,)),
+            dma, dma((16,)),
+            dma, dma((16,)),
+            dma, dma,
             dma((3,)), dma((3,)),
         ],
         compiler_params=pltpu.CompilerParams(
@@ -406,12 +431,10 @@
     queries, cache, owner, uv_weight, out_weight, norm_gain, expert_ids, gate_values,
     gate_weight, up_weight, down_weight,
 ):
-    wide = layer(
+    return layer(
         queries, cache, owner, uv_weight, out_weight, norm_gain.reshape(56, 128), expert_ids, gate_values,
         gate_weight, up_weight, down_weight.reshape(256, 7168),
     )
-    start = (lax.axis_index("expert") % 2) * 64
-    return lax.dynamic_slice_in_dim(wide, start, 448, 1)
 
 
 def solution(mesh):

time: 56.8 us -> 54.2 us (0.954)
  Pallas kernels: 55.3 us -> 52.8 us
    pallas_call x1, Pallas kernels: 55.3 us -> 52.8 us  [layer(): pl.pallas_call(layer_kernel, out_shape=jax.ShapeDtypeStruct((4, 448), BF1...]
    dynamic_slice x1 -> x0, local copies, waits for them, and re-layouts: 1.36 us -> none  [on_device(): return lax.dynamic_slice_in_dim(wide, start, 448, 1)]
    unnamed x0 -> x1, local copies, waits for them, and re-layouts: none -> 1.28 us
where the time goes in v3:
time: 54.2 us; the launch traced here: 54 us
  Pallas kernels  52.8 us (97%)
  local copies, waits for them, and re-layouts  1.28 us (2%)
    pallas_call x1, Pallas kernels, layer(): pl.pallas_call(layer_kernel, out_shape=jax.ShapeDtypeStruct((4, 448), BF1...  52.8 us
    unnamed x1, local copies, waits for them, and re-layouts  1.28 us

profile of v3, /device:TPU:1, one launch (start us, length us, event | category | flops | bytes accessed | tf_op | source)
XLA Modules:
  0.0 54.0 jit_solution(10710251736531595097)
XLA Ops:
  0.0 52.8 %layer.1 = bf16[4,448]{1,0:T(4,128)(2,1)} custom-call(bf16[4,64,576]{2,1,0:T(8,128)(2,1)} %queries_hbm.1, bf16[192,64,576]{2,1,0:T(8,128)(2,1)} %cache_hbm.1, s32[192]{0:T(256)} %owner_hbm.1, bf16[4,512,128]{2,1,0:T(8,128)(2,1)} %uv_hbm.1, bf16[512,7168]{1,0:T(8,128)(2,1)} %outw_hbm.1, f32[56,128]{1,0:T(8,128)} %bitcast.3, s32[4,8]{1,0:T(4,128)} %ids_hbm.1, ...), custom_call_target="tpu_custom_call" | custom-call | tf_op jit(solution)/shard_map/layer/pallas_call | solution.py:377
  52.8 1.3 %copy.13 = bf16[4,448]{1,0:T(4,128)(2,1)} copy(bf16[4,448]{1,0:T(4,128)(2,1)} %layer.1) | data formatting | bytes 7168

commit v4 on v3

--- a/solution.py
+++ b/solution.py
@@ -18,8 +18,6 @@
 NX = 4
 PAGES = 192
 STEP_PAGES = 32
-LOAD_PAGES = 32
-START_WEIGHTS = 0
 
 
 def hops(steps):
@@ -47,6 +45,74 @@
 
 def window_tile(e):
     return (e // 2) * 7 + (e % 2) * 3
+
+
+def attend(owner_hbm, q_hbm, cache_hbm, out_ref, start_weights, owner, q_v, q_rows, cache, sa, sb, ta, tb, m_ref, l_ref, acc_ref, sem, greet):
+    CP = STEP_PAGES
+    NCH = PAGES // CP
+    T = CP * 64
+    rows=256
+    ld0 = pltpu.make_async_copy(owner_hbm, owner, sem.at[0]); ld0.start()
+    ld1 = pltpu.make_async_copy(q_hbm, q_v, sem.at[1]); ld1.start()
+    cl = [pltpu.make_async_copy(cache_hbm.at[pl.ds(c*CP,CP)], cache.at[pl.ds(c*CP,CP)], sem.at[2+c]) for c in range(NCH)]
+    for c in cl: c.start()
+    greet()
+    ld0.wait(); ld1.wait()
+    i = lax.broadcasted_iota(jnp.int32, (rows, rows), 0)
+    j = lax.broadcasted_iota(jnp.int32, (rows, rows), 1)
+    order = (j == (i % 4) * 64 + i // 4).astype(F32).astype(BF16)
+    q_rows[...] = jnp.dot(order, q_v[...].reshape(rows, 576), preferred_element_type=F32).astype(BF16)
+    m_ref[...] = jnp.full_like(m_ref, FLOOR)
+    l_ref[...] = jnp.zeros_like(l_ref)
+    acc_ref[...] = jnp.zeros_like(acc_ref)
+    lane = lax.broadcasted_iota(jnp.int32, (8, 128), 1)
+    request = lax.broadcasted_iota(jnp.int32, (8, 128), 0) % 4
+    bufs=[sa,sb]; tops=[ta,tb]
+    def score(c):
+        cl[c].wait()
+        if c == 0:
+            start_weights()
+        keys = cache[c*CP:(c+1)*CP].reshape(T, 576)
+        s = lax.dot_general(q_rows[...], keys, (((1,), (1,)), ((), ())), preferred_element_type=F32)
+        mx=None
+        for pair in range(CP//2):
+            first = owner[c * CP + 2 * pair]
+            second = owner[c * CP + 2 * pair + 1]
+            bias=jnp.where(jnp.where(lane < 64, first, second) == request, 0.0, MASKED)
+            t = s[:, 128*pair:128*pair+128].reshape(32,8,128) * (SCORE_SCALE * LOG2E) + bias[None]
+            t = t.reshape(256,128)
+            bufs[c%2][:, 128*pair:128*pair+128] = t
+            mx = t if mx is None else jnp.maximum(mx, t)
+        tops[c%2][...] = mx
+    def weigh(c):
+        old = m_ref[...]
+        new = jnp.maximum(old, jnp.broadcast_to(jnp.max(tops[c%2][...],axis=1,keepdims=True),(256,128)))
+        alpha = jnp.exp2(old-new)
+        m_ref[...] = new
+        l = l_ref[...]*alpha
+        ps=[]
+        for pair in range(T//128):
+            p = jnp.exp2(bufs[c%2][:, 128*pair:128*pair+128] - new)
+            l = l + p
+            ps.append(p.astype(BF16))
+        l_ref[...] = l
+        vals = cache[c*CP:(c+1)*CP, :, :512].reshape(T, 512)
+        d = jnp.dot(jnp.concatenate(ps,axis=1), vals, preferred_element_type=F32)
+        acc_ref[...] = acc_ref[...]*jnp.concatenate([alpha]*4,axis=1) + d
+    score(0)
+    for c in range(NCH):
+        if c + 1 < NCH:
+            score(c + 1)
+        weigh(c)
+    total = jnp.sum(l_ref[...], axis=1, keepdims=True)
+    safe = jnp.where(total > 0.0, total, 1.0)
+    lse = jnp.where(total > 0.0, m_ref[...] + jnp.log2(safe), FLOOR)
+    wide = lax.broadcasted_iota(jnp.int32, (256, 128), 1)
+    coded = jnp.zeros((256, 128), F32)
+    for at, piece in enumerate(split_bf16(lse, 3)):
+        coded = jnp.where(wide == at, piece, coded)
+    out_ref[:, :, :512] = (acc_ref[...] / safe).astype(BF16).reshape(16, 16, 512)
+    out_ref[:, :, 512:] = coded.astype(BF16).reshape(16, 16, 128)
 
 
 def layer_kernel(
@@ -81,17 +147,8 @@
             src_ref=src, dst_ref=dst, send_sem=send, recv_sem=recv, device_id=to, device_id_type=MESH
         )
 
-    owner_load = pltpu.make_async_copy(owner_hbm, owner, load_sem.at[0])
-    queries_load = pltpu.make_async_copy(queries_hbm, queries, load_sem.at[1])
-    owner_load.start()
-    queries_load.start()
-    cache_loads = []
-    for c in range(PAGES // LOAD_PAGES):
-        at = pl.ds(c * LOAD_PAGES, LOAD_PAGES)
-        cache_loads.append(pltpu.make_async_copy(cache_hbm.at[at], cache.at[at], cache_sem.at[c]))
-        cache_loads[-1].start()
     loads = [
-        pltpu.make_async_copy(src, dst, load_sem.at[n + 2])
+        pltpu.make_async_copy(src, dst, load_sem.at[n])
         for n, (src, dst) in enumerate(
             [(uv_hbm, uv), (outw_hbm, outw), (gain_hbm, gain), (ids_hbm, ids_ref), (values_hbm, values_ref),
              (gate_hbm, gate), (up_hbm, up), (down_hbm, down)]
@@ -99,81 +156,19 @@
     ]
     barrier = pltpu.get_barrier_semaphore()
 
-    def greet(offsets):
-        for offset in offsets:
+    def greet():
+        pl.semaphore_signal(barrier, inc=1, device_id=sibling, device_id_type=MESH)
+        for offset in OFFSETS:
             pl.semaphore_signal(barrier, inc=1, device_id=device(*offset), device_id_type=MESH)
 
-    pl.semaphore_signal(barrier, inc=1, device_id=sibling, device_id_type=MESH)
-    greet(OFFSETS)
-
-    owner_load.wait()
-    queries_load.wait()
-    rows = 256
-    i = lax.broadcasted_iota(jnp.int32, (rows, rows), 0)
-    j = lax.broadcasted_iota(jnp.int32, (rows, rows), 1)
-    order = (j == (i % 4) * 64 + i // 4).astype(F32).astype(BF16)
-    q_rows[...] = jnp.dot(order, queries[...].reshape(rows, 576), preferred_element_type=F32).astype(BF16)
-    lane8 = lax.broadcasted_iota(jnp.int32, (8, 128), 1)
-    request = lax.broadcasted_iota(jnp.int32, (8, 128), 0) % 4
-    tokens = STEP_PAGES * 64
-    steps = PAGES // STEP_PAGES
-    per = STEP_PAGES // LOAD_PAGES
-    peak_ref[...] = jnp.full((rows, 128), FLOOR, F32)
-    total_ref[...] = jnp.zeros((rows, 128), F32)
-    value_ref[...] = jnp.zeros((rows, 512), F32)
-    scores = (scores_even, scores_odd)
-    tops = (top_even, top_odd)
-
-    def score(c):
-        for load in cache_loads[c * per : (c + 1) * per]:
-            load.wait()
-        if c == START_WEIGHTS:
-            for load in loads:
-                load.start()
-        keys = cache[c * STEP_PAGES : (c + 1) * STEP_PAGES].reshape(tokens, 576)
-        raw = lax.dot_general(q_rows[...], keys, (((1,), (1,)), ((), ())), preferred_element_type=F32)
-        top = None
-        for pair in range(STEP_PAGES // 2):
-            first = owner[c * STEP_PAGES + 2 * pair]
-            second = owner[c * STEP_PAGES + 2 * pair + 1]
-            bias = jnp.where(jnp.where(lane8 < 64, first, second) == request, 0.0, MASKED)
-            tile = raw[:, 128 * pair : 128 * pair + 128].reshape(32, 8, 128) * (SCORE_SCALE * LOG2E) + bias[None]
-            tile = tile.reshape(rows, 128)
-            scores[c % 2][:, 128 * pair : 128 * pair + 128] = tile
-            top = tile if top is None else jnp.maximum(top, tile)
-        tops[c % 2][...] = top
-
-    def weigh(c):
-        old = peak_ref[...]
-        top = jnp.max(tops[c % 2][...], axis=1, keepdims=True)
-        peak = jnp.maximum(old, jnp.broadcast_to(top, (rows, 128)))
-        alpha = jnp.exp2(old - peak)
-        peak_ref[...] = peak
-        total = total_ref[...] * alpha
-        probs = []
-        for pair in range(STEP_PAGES // 2):
-            prob = jnp.exp2(scores[c % 2][:, 128 * pair : 128 * pair + 128] - peak)
-            total = total + prob
-            probs.append(prob.astype(BF16))
-        total_ref[...] = total
-        values = cache[c * STEP_PAGES : (c + 1) * STEP_PAGES, :, :512].reshape(tokens, 512)
-        added = jnp.dot(jnp.concatenate(probs, axis=1), values, preferred_element_type=F32)
-        value_ref[...] = value_ref[...] * jnp.concatenate([alpha] * 4, axis=1) + added
-
-    score(0)
-    for c in range(steps):
-        if c + 1 < steps:
-            score(c + 1)
-        weigh(c)
-    total = jnp.sum(total_ref[...], axis=1, keepdims=True)
-    safe = jnp.where(total > 0.0, total, 1.0)
-    lse = jnp.where(total > 0.0, peak_ref[...] + jnp.log2(safe), FLOOR)
-    wide = lax.broadcasted_iota(jnp.int32, (rows, 128), 1)
-    coded = jnp.zeros((rows, 128), F32)
-    for at, piece in enumerate(split_bf16(lse, 3)):
-        coded = jnp.where(wide == at, piece, coded)
-    part_send[:, :, :512] = (value_ref[...] / safe).astype(BF16).reshape(16, 16, 512)
-    part_send[:, :, 512:] = coded.astype(BF16).reshape(16, 16, 128)
+    def start_weights():
+        for load in loads:
+            load.start()
+
+    attend(
+        owner_hbm, queries_hbm, cache_hbm, part_send, start_weights, owner, queries, q_rows, cache,
+        scores_even, scores_odd, top_even, top_odd, peak_ref, total_ref, value_ref, cache_sem, greet,
+    )
 
     pl.semaphore_wait(barrier, len(OFFSETS) + 1)
     sends = []
@@ -410,7 +405,7 @@
             pltpu.VMEM((16, 64, 128), BF16),
             pltpu.VMEM((16, NX, 16, 128), BF16),
             pltpu.VMEM((16, NX, 16, 128), BF16),
-            dma((10,)), dma((PAGES // LOAD_PAGES,)),
+            dma((8,)), dma((2 + PAGES // STEP_PAGES,)),
             dma, dma,
             dma, dma,
             dma((3,)), dma((4,)),

time: 54.2 us -> 51.2 us (0.945)
  Pallas kernels: 52.8 us -> 49.8 us
    pallas_call x1, Pallas kernels: 52.8 us -> 49.8 us  [layer(): pl.pallas_call(layer_kernel, out_shape=jax.ShapeDtypeStruct((4, 448), BF1...]
where the time goes in v4:
time: 51.2 us; the launch traced here: 51.1 us
  Pallas kernels  49.8 us (97%)
  local copies, waits for them, and re-layouts  1.28 us (2%)
    pallas_call x1, Pallas kernels, layer(): pl.pallas_call(layer_kernel, out_shape=jax.ShapeDtypeStruct((4, 448), BF1...  49.8 us
    unnamed x1, local copies, waits for them, and re-layouts  1.28 us

profile of v4, /device:TPU:1, one launch (start us, length us, event | category | flops | bytes accessed | tf_op | source)
XLA Modules:
  0.0 51.1 jit_solution(2456279887314185760)
XLA Ops:
  0.0 49.8 %layer.1 = bf16[4,448]{1,0:T(4,128)(2,1)} custom-call(bf16[4,64,576]{2,1,0:T(8,128)(2,1)} %queries_hbm.1, bf16[192,64,576]{2,1,0:T(8,128)(2,1)} %cache_hbm.1, s32[192]{0:T(256)} %owner_hbm.1, bf16[4,512,128]{2,1,0:T(8,128)(2,1)} %uv_hbm.1, bf16[512,7168]{1,0:T(8,128)(2,1)} %outw_hbm.1, f32[56,128]{1,0:T(8,128)} %bitcast.3, s32[4,8]{1,0:T(4,128)} %ids_hbm.1, ...), custom_call_target="tpu_custom_call" | custom-call | tf_op jit(solution)/shard_map/layer/pallas_call | solution.py:372
  49.8 1.3 %copy.13 = bf16[4,448]{1,0:T(4,128)(2,1)} copy(bf16[4,448]{1,0:T(4,128)(2,1)} %layer.1) | data formatting | bytes 7168

commit v5 on v4

--- a/solution.py
+++ b/solution.py
@@ -30,7 +30,7 @@
 )
 PLANE = [d[1:] for d in OFFSETS if d[0] == 0]
 LAG = 8
-AHEAD = 2
+AHEAD = 5
 PAIRS = [(0, 0), (0, 1), (1, 0), (3, 0), (1, 1), (3, 1), (2, 0), (2, 1)]
 
 

time: 51.2 us -> 50.7 us (level)
    pallas_call x1, Pallas kernels: 49.8 us -> 49.3 us  [layer(): pl.pallas_call(layer_kernel, out_shape=jax.ShapeDtypeStruct((4, 448), BF1...]
where the time goes in v5:
time: 50.7 us; the launch traced here: 50.6 us
  Pallas kernels  49.3 us (97%)
  local copies, waits for them, and re-layouts  1.28 us (3%)
    pallas_call x1, Pallas kernels, layer(): pl.pallas_call(layer_kernel, out_shape=jax.ShapeDtypeStruct((4, 448), BF1...  49.3 us
    unnamed x1, local copies, waits for them, and re-layouts  1.28 us

profile of v5, /device:TPU:1, one launch (start us, length us, event | category | flops | bytes accessed | tf_op | source)
XLA Modules:
  0.0 50.6 jit_solution(456482721313583282)
XLA Ops:
  0.0 49.3 %layer.1 = bf16[4,448]{1,0:T(4,128)(2,1)} custom-call(bf16[4,64,576]{2,1,0:T(8,128)(2,1)} %queries_hbm.1, bf16[192,64,576]{2,1,0:T(8,128)(2,1)} %cache_hbm.1, s32[192]{0:T(256)} %owner_hbm.1, bf16[4,512,128]{2,1,0:T(8,128)(2,1)} %uv_hbm.1, bf16[512,7168]{1,0:T(8,128)(2,1)} %outw_hbm.1, f32[56,128]{1,0:T(8,128)} %bitcast.3, s32[4,8]{1,0:T(4,128)} %ids_hbm.1, ...), custom_call_target="tpu_custom_call" | custom-call | tf_op jit(solution)/shard_map/layer/pallas_call | solution.py:372
  49.3 1.3 %copy.13 = bf16[4,448]{1,0:T(4,128)(2,1)} copy(bf16[4,448]{1,0:T(4,128)(2,1)} %layer.1) | data formatting | bytes 7168
